TPU v7x, 256 devices: a whole 4x4x8 slice. The times are simulated.
256 devices in a mesh: seq: 8 (over x, core), head: 32 (over y, z).
Axes of the slice: x: 4, y: 4, z: 8, core: 2. Of those that a mesh axis runs over, the one named last changes fastest.
Arguments:
- inputs: bfloat16 [81920, 8192], P(('seq', 'head')), may hold values from -6 to 6
- b_panel: bfloat16 [81920, 128], P(('seq', 'head')), may hold values from -0.52734375 to 0.52734375
- c_panel: bfloat16 [81920, 128], P(('seq', 'head')), may hold values from -0.52734375 to 0.52734375
- dt_raw: bfloat16 [81920, 128], P(('seq', 'head')), may hold values from -3 to 3
- dt_bias: float32 [128], replicated, may hold values from -3.5 to 0.5
- a_log: float32 [128], replicated, may hold values from -12 to 1
- d_skip: float32 [128], replicated, may hold values from 0.5 to 1.5
Outputs:
- mixed: bfloat16 [81920, 8192], P(('seq', 'head'))
All inputs are finite; a program needn't handle non-finite values.
Results may differ from a plain program's by a relative error of at most 0.0051.
Values may be sent and summed in bfloat16 or wider, within the bound.
A program may use at most 128 MiB of HBM per device.

v0:
```python
import jax
import jax.numpy as jnp
from jax import lax
from jax.sharding import PartitionSpec as P

HEADS = 128
HDIM = 64
DSTATE = 128
SPAN = 256


def passed_along(block, axis, distance):
    devices = range(lax.axis_size(axis))
    route = [(i - distance, i) for i in devices if i - distance in devices]
    return lax.ppermute(block, axis, route)


def head_terms(cumulative, delta_head, tokens_head, scores, b_spans):
    positions = jnp.arange(SPAN, dtype=jnp.int32)
    causal_mask = positions[:, None] >= positions[None, :]
    spread = cumulative[:, :, None] - cumulative[:, None, :]
    decays = jnp.exp(jnp.where(causal_mask[None], spread, -1e30))
    weights = (scores * decays * delta_head[:, None, :]).astype(jnp.bfloat16)
    within = jnp.einsum("kts,ksp->ktp", weights, tokens_head, preferred_element_type=jnp.float32)
    ending = cumulative[:, -1:]
    scaled_b = (b_spans * (jnp.exp(ending - cumulative) * delta_head)[:, :, None]).astype(
        jnp.bfloat16
    )
    span_state = jnp.einsum(
        "ksn,ksp->knp", scaled_b, tokens_head, preferred_element_type=jnp.float32
    )
    return (within, span_state, jnp.exp(ending[:, 0]))


def on_device(inputs, b_panel, c_panel, dt_raw, dt_bias, a_log, d_skip):
    groups = lax.axis_size("head")
    local_heads = HEADS // groups
    tokens, raw_steps = (
        lax.all_to_all(inputs, "head", split_axis=1, concat_axis=0, tiled=True),
        lax.all_to_all(dt_raw, "head", split_axis=1, concat_axis=0, tiled=True),
    )
    b_whole, c_whole = (
        lax.all_gather(b_panel, "head", axis=0, tiled=True),
        lax.all_gather(c_panel, "head", axis=0, tiled=True),
    )
    length = tokens.shape[0]
    blocks = length // SPAN
    first_head = lax.axis_index("head") * local_heads
    bias_here = lax.dynamic_slice_in_dim(dt_bias, first_head, local_heads)
    alog_here = lax.dynamic_slice_in_dim(a_log, first_head, local_heads)
    skip_here = lax.dynamic_slice_in_dim(d_skip, first_head, local_heads)
    delta = jax.nn.softplus(raw_steps.astype(jnp.float32) + bias_here[None, :])
    rates = -jnp.exp(alog_here)[None, :] * delta
    cumulative = jnp.cumsum(rates.reshape(blocks, SPAN, local_heads), axis=1)
    delta_blocks = delta.reshape(blocks, SPAN, local_heads)
    b_spans = b_whole.reshape(blocks, SPAN, DSTATE)
    c_spans = c_whole.reshape(blocks, SPAN, DSTATE)
    scores = jnp.einsum("ktn,ksn->kts", c_spans, b_spans, preferred_element_type=jnp.float32)
    tokens_all = tokens.reshape(blocks, SPAN, local_heads, HDIM)

    def one_head(head):
        tokens_head = lax.dynamic_index_in_dim(tokens_all, head, 2, keepdims=False)
        cum_head = lax.dynamic_index_in_dim(cumulative, head, 2, keepdims=False)
        delta_head = lax.dynamic_index_in_dim(delta_blocks, head, 2, keepdims=False)
        return head_terms(cum_head, delta_head, tokens_head, scores, b_spans)

    within, span_state, span_decay = lax.map(one_head, jnp.arange(local_heads, dtype=jnp.int32))

    def advance(running, pieces):
        state_now, product = running
        factor, update = pieces
        return (
            (factor[:, None, None] * state_now + update, product * factor),
            (state_now, product),
        )

    start_state = (
        jnp.zeros((local_heads, DSTATE, HDIM), jnp.float32),
        jnp.ones((local_heads,), jnp.float32),
    )
    finals, befores = lax.scan(
        advance, start_state, (jnp.transpose(span_decay), jnp.moveaxis(span_state, 1, 0))
    )
    final_state, total_decay = finals
    entering, prefix_decay = befores
    incoming = jnp.zeros((local_heads, DSTATE, HDIM), jnp.float32)
    for turn_index in range(lax.axis_size("seq") - 1):
        leaving = total_decay[:, None, None] * incoming + final_state
        incoming = passed_along(leaving, "seq", 1)
    states = entering + prefix_decay[:, :, None, None] * incoming[None]
    states_b = states.astype(jnp.bfloat16)
    carried = jnp.einsum("ktn,khnp->kthp", c_spans, states_b, preferred_element_type=jnp.float32)
    ordered = jnp.transpose(within, (1, 2, 0, 3))
    combined = (
        ordered
        + carried * jnp.exp(cumulative)[..., None]
        + skip_here[:, None] * tokens_all.astype(jnp.float32)
    )
    result = combined.astype(jnp.bfloat16).reshape(length, local_heads * HDIM)
    return lax.all_to_all(result, "head", split_axis=0, concat_axis=1, tiled=True)


def solution(mesh):
    return jax.shard_map(
        on_device,
        mesh=mesh,
        in_specs=(
            P(("seq", "head"), None),
            P(("seq", "head"), None),
            P(("seq", "head"), None),
            P(("seq", "head"), None),
            P(),
            P(),
            P(),
        ),
        out_specs=P(("seq", "head"), None),
        check_vma=False,
    )
```

profile of v0, /device:TPU:1, one launch (start us, length us, event | category | flops | bytes accessed | tf_op | source)
XLA Modules:
  0.0 608.3 jit_solution(6843153276479366639)
XLA Ops:
  8.9 12.0 %all-to-all-start = ((bf16[320,32,4]{0,2,1:T(4,128)(2,1)}), bf16[320,32,4]{0,2,1:T(4,128)(2,1)S(1)}, u32[]{:S(2)}, u32[]{:S(2)}) async-start(bf16[320,32,4]{0,2,1:T(4,128)(2,1)} %all_to_all.36), calls=%async_computation | async-start | bytes 196608 | tf_op jit(solution)/shard_map/all_to_all | solution.py:40
  21.0 5.4 copy.114
  30.0 5.9 all-to-all-start.1
  40.0 76.0 %all-gather.3.cloned.1.call-done = bf16[10240,128]{1,0:T(8,128)(2,1)} async-done(((bf16[320,128]{1,0:T(8,128)(2,1)}), bf16[10240,128]{1,0:T(8,128)(2,1)}) %all-gather.3.cloned.1.call-update) | async-done | bytes 2621456 | tf_op jit(solution)/shard_map/all_gather | solution.py:44
  116.0 90.1 %all-gather.5.cloned.1.call-done = bf16[10240,128]{1,0:T(8,128)(2,1)} async-done(((bf16[320,128]{1,0:T(8,128)(2,1)}), bf16[10240,128]{1,0:T(8,128)(2,1)}) %all-gather.5.cloned.1.call-update) | async-done | bytes 2621456 | tf_op jit(solution)/shard_map/all_gather | solution.py:43
  206.1 7.9 %fusion.19 = f32[40,256,256]{2,1,0:T(8,128)} fusion(bf16[40,256,128]{2,1,0:T(8,128)(2,1)} %bitcast.108, bf16[40,256,128]{2,1,0:T(8,128)(2,1)} %bitcast.111), kind=kOutput, calls=%fused_computation.52 | convolution fusion | flops 671088640 | bytes 15728640 | tf_op jit(solution)/shard_map/ktn,ksn->kts/dot_general | solution.py:58
  214.0 8.7 %copy.81 = bf16[32,320,256]{1,0,2:T(8,128)(2,1)} copy(bf16[32,320,256]{2,1,0:T(8,128)(2,1)} %bitcast.12) | data formatting | bytes 10485760 | tf_op jit(solution)/shard_map/all_to_all | solution.py:39
  222.7 13.2 %reshape.98 = bf16[40,256,4,64]{1,0,3,2:T(8,128)(2,1)} reshape(bf16[32,320,256]{1,0,2:T(8,128)(2,1)} %copy.81) | data formatting | bytes 10485760 | tf_op jit(solution)/shard_map/reshape | solution.py:59
  235.8 56.5 %while.31 = (s32[]{:T(128)}, f32[4,40,256,64]{2,3,0,1:T(8,128)}, f32[4,40,128,64]{2,3,1,0:T(8,128)}, f32[4,40]{1,0:T(4,128)S(1)}, s32[4]{0:T(128)S(1)}, /*index=...) while((s32[]{:T(128)}, f32[4,40,256,64]{2,3,0,1:T(8,128)}, ...), condition=%wide.region_3.4_spmd, body=%wide.region_2.3_spmd.sunk | while | flops 520441856 | bytes 22825084 | solution.py:67
  239.9 6.8 %bitcast_dynamic-update-slice_fusion.4 = f32[4,40,256,64]{2,3,0,1:T(8,128)} fusion(f32[4,40,256,64]{2,3,0,1:T(8,128)} %get-tuple-element.365, s32[]{:T(128)} %get-tuple-element.364, f32[40,256,256]{2,1,0:T(8,128)} %get-tuple-element.383, f32[40,256]{1,0:T(8,128)S(1)} %get-tuple-element.338, f32[40,256]{1,0:T(8,128)S(1)} %dynamic-slice_bitcast_fusion.3, ...), kind=kOutput, calls=%fused_computation.12.clone.1 | convolution fusion | flops 348651520 | bytes 14606848 | tf_op jit(solution)/shard_map/while/body/eval_jaxpr/kts,ksp->ktp/dot_general | solution.py:24
  254.0 6.8 %bitcast_dynamic-update-slice_fusion.4 = f32[4,40,256,64]{2,3,0,1:T(8,128)} fusion(f32[4,40,256,64]{2,3,0,1:T(8,128)} %get-tuple-element.365, s32[]{:T(128)} %get-tuple-element.364, f32[40,256,256]{2,1,0:T(8,128)} %get-tuple-element.383, f32[40,256]{1,0:T(8,128)S(1)} %get-tuple-element.338, f32[40,256]{1,0:T(8,128)S(1)} %dynamic-slice_bitcast_fusion.3, ...), kind=kOutput, calls=%fused_computation.12.clone.1 | convolution fusion | flops 348651520 | bytes 14606848 | tf_op jit(solution)/shard_map/while/body/eval_jaxpr/kts,ksp->ktp/dot_general | solution.py:24
  268.1 6.9 %bitcast_dynamic-update-slice_fusion.4 = f32[4,40,256,64]{2,3,0,1:T(8,128)} fusion(f32[4,40,256,64]{2,3,0,1:T(8,128)} %get-tuple-element.365, s32[]{:T(128)} %get-tuple-element.364, f32[40,256,256]{2,1,0:T(8,128)} %get-tuple-element.383, f32[40,256]{1,0:T(8,128)S(1)} %get-tuple-element.338, f32[40,256]{1,0:T(8,128)S(1)} %dynamic-slice_bitcast_fusion.3, ...), kind=kOutput, calls=%fused_computation.12.clone.1 | convolution fusion | flops 348651520 | bytes 14606848 | tf_op jit(solution)/shard_map/while/body/eval_jaxpr/kts,ksp->ktp/dot_general | solution.py:24
  282.2 6.8 %bitcast_dynamic-update-slice_fusion.4 = f32[4,40,256,64]{2,3,0,1:T(8,128)} fusion(f32[4,40,256,64]{2,3,0,1:T(8,128)} %get-tuple-element.365, s32[]{:T(128)} %get-tuple-element.364, f32[40,256,256]{2,1,0:T(8,128)} %get-tuple-element.383, f32[40,256]{1,0:T(8,128)S(1)} %get-tuple-element.338, f32[40,256]{1,0:T(8,128)S(1)} %dynamic-slice_bitcast_fusion.3, ...), kind=kOutput, calls=%fused_computation.12.clone.1 | convolution fusion | flops 348651520 | bytes 14606848 | tf_op jit(solution)/shard_map/while/body/eval_jaxpr/kts,ksp->ktp/dot_general | solution.py:24
  292.3 8.5 %copy.85 = f32[4,40,128,64]{3,2,0,1:T(8,128)} copy(f32[4,40,128,64]{2,3,1,0:T(8,128)} %get-tuple-element.101) | data formatting | bytes 10485760 | tf_op jit(solution)/shard_map/while | solution.py:67
  300.9 74.1 %while.32 = (s32[]{:T(128)}, f32[4,128,64]{2,1,0:T(8,128)S(1)}, f32[4]{0:T(128)S(1)}, f32[40,4,128,64]{3,2,1,0:T(8,128)}, f32[40,4]{1,0:T(8,128)S(1)}, /*index=5...) while((s32[]{:T(128)}, f32[4,128,64]{2,1,0:T(8,128)S(1)}, ...), condition=%wide.region_5.6_spmd.clone, body=%wide.region_4.5_spmd.clone.sunk | while | flops 131083 | bytes 787189 | solution.py:81
  375.1 7.2 %collective-permute-start = (f32[4,128,64]{2,1,0:T(8,128)S(1)}, f32[4,128,64]{2,1,0:T(8,128)S(1)}, u32[]{:S(2)}, u32[]{:S(2)}) collective-permute-start(f32[4,128,64]{2,1,0:T(8,128)S(1)} %broadcast_add_fusion), channel_id=1, source_target_pairs={{0,32},{32,64},{64,96},{96,128},{128,160},{160,192},{192,224},{1,3... | collective-permute-start | bytes 393224 | tf_op jit(solution)/shard_map/ppermute | solution.py:15
  385.6 4.4 collective-permute-start.1
  393.4 4.4 collective-permute-start.2
  416.8 4.4 collective-permute-start.5
  424.6 4.6 collective-permute-start.6
  432.3 14.5 %fusion.12 = bf16[40,256,4,64]{1,3,2,0:T(8,128)(2,1)} fusion(f32[4,40,256,64]{2,3,0,1:T(8,128)} %get-tuple-element.99, bf16[40,256,4,64]{1,0,3,2:T(8,128)(2,1)} %get-tuple-element.419, f32[4]{0:T(128)S(1)} %dynamic_slice.34, f32[40,256,4]{1,2,0:T(4,128)S(1)} %copy.87, bf16[40,256,128,1]{2,1,3,0:T(8,128)(2,1)S(1)} %bitcast.109, ...), kind=kOutput, calls=%fused_computation.28 | convolution fusion | flops 690749440 | bytes 29131408 | tf_op jit(solution)/shard_map/ktn,khnp->kthp/dot_general | solution.py:92
  446.8 15.3 %copy.94 = bf16[40,256,4,64]{3,2,1,0:T(4,128)(2,1)} copy(bf16[40,256,4,64]{1,3,2,0:T(8,128)(2,1)} %fusion.12) | data formatting | bytes 10485760 | tf_op jit(solution)/shard_map/all_to_all | solution.py:100
  462.1 15.7 %reshape.101 = bf16[32,320,256]{2,1,0:T(8,128)(2,1)} reshape(bf16[40,256,4,64]{3,2,1,0:T(4,128)(2,1)} %copy.94) | data formatting | bytes 10485760 | tf_op jit(solution)/shard_map/all_to_all | solution.py:100
  477.8 120.6 %all_to_all.48 = bf16[32,320,256]{2,1,0:T(8,128)(2,1)S(1)} all-to-all(bf16[32,320,256]{2,1,0:T(8,128)(2,1)} %reshape.101), channel_id=1, replica_groups=mesh['seq'=8,'head'=32] {'head'}, dimensions={0} | all-to-all | bytes 10485760 | tf_op jit(solution)/shard_map/all_to_all | solution.py:100
  (252 shorter events, 140.7 us)
Async XLA Ops:
  6.5 109.5 %all-gather.3.cloned.1.call-start = ((), (), s32[]{:S(2)}) async-start(), calls=%async_computation.3 | async-start | bytes 2703360 | tf_op jit(solution)/shard_map/all_gather | solution.py:44
  8.9 21.1 %all-to-all-start = ((bf16[320,32,4]{0,2,1:T(4,128)(2,1)}), bf16[320,32,4]{0,2,1:T(4,128)(2,1)S(1)}, u32[]{:S(2)}, u32[]{:S(2)}) async-start(bf16[320,32,4]{0,2,1:T(4,128)(2,1)} %all_to_all.36), calls=%async_computation | async-start | bytes 196608 | tf_op jit(solution)/shard_map/all_to_all | solution.py:40
  30.0 6.7 %copy-start.2 = (f32[128]{0:T(128)S(1)}, f32[128]{0:T(128)}, u32[]{:S(2)}) copy-start(f32[128]{0:T(128)} %param.15) | copy-start | bytes 1540
  30.0 6.8 %copy-start.3 = (f32[128]{0:T(128)S(1)}, f32[128]{0:T(128)}, u32[]{:S(2)}) copy-start(f32[128]{0:T(128)} %param.16) | copy-start | bytes 1540
  30.0 184.0 %all-to-all-start.1 = ((bf16[320,32,256]{2,0,1:T(8,128)(2,1)}), bf16[320,32,256]{2,0,1:T(8,128)(2,1)}, u32[]{:S(2)}, u32[]{:S(2)}) async-start(bf16[320,32,256]{2,0,1:T(8,128)(2,1)} %bitcast.105), calls=%async_computation.1 | async-start | bytes 10485760 | tf_op jit(solution)/shard_map/all_to_all | solution.py:39
  35.9 170.2 %all-gather.5.cloned.1.call-start = ((), (), s32[]{:S(2)}) async-start(), calls=%async_computation.4 | async-start | bytes 2703360 | tf_op jit(solution)/shard_map/all_gather | solution.py:43
  222.7 13.2 %copy-start.1 = (bf16[10240,128]{1,0:T(8,128)(2,1)S(1)}, bf16[10240,128]{1,0:T(8,128)(2,1)}, u32[]{:S(2)}) copy-start(bf16[10240,128]{1,0:T(8,128)(2,1)} %all-gather.5.cloned.1.call-done) | copy-start | bytes 7864324
  300.9 120.3 %copy-start.4 = (f32[128]{0:T(128)S(1)}, f32[128]{0:T(128)}, u32[]{:S(2)}) copy-start(f32[128]{0:T(128)} %param.17) | copy-start | bytes 1540
  300.9 131.4 %copy-start = (bf16[10240,128]{1,0:T(8,128)(2,1)S(1)}, bf16[10240,128]{1,0:T(8,128)(2,1)}, u32[]{:S(2)}) copy-start(bf16[10240,128]{1,0:T(8,128)(2,1)} %all-gather.3.cloned.1.call-done) | copy-start | bytes 7864324
  375.1 10.5 %collective-permute-start = (f32[4,128,64]{2,1,0:T(8,128)S(1)}, f32[4,128,64]{2,1,0:T(8,128)S(1)}, u32[]{:S(2)}, u32[]{:S(2)}) collective-permute-start(f32[4,128,64]{2,1,0:T(8,128)S(1)} %broadcast_add_fusion), channel_id=1, source_target_pairs={{0,32},{32,64},{64,96},{96,128},{128,160},{160,192},{192,224},{1,3... | collective-permute-start | bytes 393224 | tf_op jit(solution)/shard_map/ppermute | solution.py:15
  385.6 7.7 %collective-permute-start.1 = (f32[4,128,64]{2,1,0:T(8,128)S(1)}, f32[4,128,64]{2,1,0:T(8,128)S(1)}, u32[]{:S(2)}, u32[]{:S(2)}) collective-permute-start(f32[4,128,64]{2,1,0:T(8,128)S(1)} %multiply_add_fusion.5), channel_id=1, source_target_pairs={{0,32},{32,64},{64,96},{96,128},{128,160},{160,192},{192,224},{1,3... | collective-permute-start | bytes 393224 | tf_op jit(solution)/shard_map/ppermute | solution.py:15
  393.4 7.7 %collective-permute-start.2 = (f32[4,128,64]{2,1,0:T(8,128)S(1)}, f32[4,128,64]{2,1,0:T(8,128)S(1)}, u32[]{:S(2)}, u32[]{:S(2)}) collective-permute-start(f32[4,128,64]{2,1,0:T(8,128)S(1)} %multiply_add_fusion.4), channel_id=1, source_target_pairs={{0,32},{32,64},{64,96},{96,128},{128,160},{160,192},{192,224},{1,3... | collective-permute-start | bytes 393224 | tf_op jit(solution)/shard_map/ppermute | solution.py:15
  401.2 7.7 %collective-permute-start.3 = (f32[4,128,64]{2,1,0:T(8,128)S(1)}, f32[4,128,64]{2,1,0:T(8,128)S(1)}, u32[]{:S(2)}, u32[]{:S(2)}) collective-permute-start(f32[4,128,64]{2,1,0:T(8,128)S(1)} %multiply_add_fusion.3), channel_id=1, source_target_pairs={{0,32},{32,64},{64,96},{96,128},{128,160},{160,192},{192,224},{1,3... | collective-permute-start | bytes 393224 | tf_op jit(solution)/shard_map/ppermute | solution.py:15
  409.0 7.7 %collective-permute-start.4 = (f32[4,128,64]{2,1,0:T(8,128)S(1)}, f32[4,128,64]{2,1,0:T(8,128)S(1)}, u32[]{:S(2)}, u32[]{:S(2)}) collective-permute-start(f32[4,128,64]{2,1,0:T(8,128)S(1)} %multiply_add_fusion.2), channel_id=1, source_target_pairs={{0,32},{32,64},{64,96},{96,128},{128,160},{160,192},{192,224},{1,3... | collective-permute-start | bytes 393224 | tf_op jit(solution)/shard_map/ppermute | solution.py:15
  416.8 7.7 %collective-permute-start.5 = (f32[4,128,64]{2,1,0:T(8,128)S(1)}, f32[4,128,64]{2,1,0:T(8,128)S(1)}, u32[]{:S(2)}, u32[]{:S(2)}) collective-permute-start(f32[4,128,64]{2,1,0:T(8,128)S(1)} %multiply_add_fusion.1), channel_id=1, source_target_pairs={{0,32},{32,64},{64,96},{96,128},{128,160},{160,192},{192,224},{1,3... | collective-permute-start | bytes 393224 | tf_op jit(solution)/shard_map/ppermute | solution.py:15
  424.6 7.7 %collective-permute-start.6 = (f32[4,128,64]{2,1,0:T(8,128)S(1)}, f32[4,128,64]{2,1,0:T(8,128)S(1)}, u32[]{:S(2)}, u32[]{:S(2)}) collective-permute-start(f32[4,128,64]{2,1,0:T(8,128)S(1)} %multiply_add_fusion), channel_id=1, source_target_pairs={{0,32},{32,64},{64,96},{96,128},{128,160},{160,192},{192,224},{1,3... | collective-permute-start | bytes 393224 | tf_op jit(solution)/shard_map/ppermute | solution.py:15
Sparse Core Ops, SparseCore 0:
  9.9 106.0 all-gather.2
  118.6 87.4 all-gather.4
where the time goes:
time: 614 us; the launch traced here: 608 us
  waiting for transfers between devices  194 us (32%)
  blocking collectives  121 us (20%)
  local copies, waits for them, and re-layouts  82.6 us (13%)
  other arithmetic  75.7 us (12%)
  matrix products  62.4 us (10%)
  starting transfers between devices  51.6 us (8%)
  between operations  13.7 us (2%)
  loops' own time  7.91 us (1%)
    all_to_all x1, blocking collectives, on_device(): lax.all_to_all(result, 'head', split_axis=0, concat_axis=1, tiled=True)  121 us
    all_gather x1, waiting for transfers between devices, on_device(): lax.all_gather(b_panel, 'head', axis=0, tiled=True)  90.1 us
    all_gather x1, waiting for transfers between devices, on_device(): lax.all_gather(c_panel, 'head', axis=0, tiled=True)  76 us
    add x40, other arithmetic, advance(): factor[:, None, None] * state_now + update  41.8 us
    all_to_all x3, local copies, waits for them, and re-layouts, on_device(): lax.all_to_all(result, 'head', split_axis=0, concat_axis=1, tiled=True)  34.1 us
    ppermute x7, starting transfers between devices, passed_along(): return lax.ppermute(block, axis, route)  33.7 us
    dynamic_update_slice x40, other arithmetic, on_device(): lax.scan(advance, start_state, (jnp.transpose(span_decay), jnp.moveaxis(s...  29.2 us
    dot_general x4, matrix products, head_terms(): jnp.einsum('kts,ksp->ktp', weights, tokens_head, preferred_element_type=j...  27.3 us
  transfers between devices with their start and end apart: 11, of which 10 were waited for; matrix products, arithmetic and copies ran while one was open for 3% of the time, Pallas kernels for 0%

commit v1 on v0

v1 whole, which is shorter than its diff:
```python
import functools

import jax
import jax.numpy as jnp
from jax import lax
from jax.experimental import pallas as pl
from jax.experimental.pallas import tpu as pltpu
from jax.sharding import PartitionSpec as P

HEADS = 128
HDIM = 64
DSTATE = 128
TOK = 320
PIECES = HEADS // 2
LOG2E = 1.4426950408889634
F32 = jnp.float32
BF16 = jnp.bfloat16
VMEM_LIMIT = 56 * 1024 * 1024


def state_kernel(x_ref, b_ref, c_ref, dt_ref, bias_ref, alog_ref, l_ref, a_ref, rt_ref, sm_ref, g_ref, bt_ref):
    step = pl.program_id(0)

    @pl.when(step == 0)
    def _():
        v = dt_ref[...].astype(F32) + bias_ref[...]
        delta = jnp.maximum(v, 0.0) + jnp.log(1.0 + jnp.exp(-jnp.abs(v)))
        rates = (-LOG2E) * jnp.exp(alog_ref[...]) * delta
        row = lax.broadcasted_iota(jnp.int32, (TOK, TOK), 0)
        col = lax.broadcasted_iota(jnp.int32, (TOK, TOK), 1)
        lower = (row >= col).astype(F32)
        a = jnp.dot(lower, rates, precision=lax.Precision.HIGHEST, preferred_element_type=F32)
        a_ref[...] = a
        r = a - jnp.log2(delta)
        rt_ref[...] = r.T
        g_ref[...] = (jnp.exp2(a[TOK - 1 : TOK, :] - a) * delta).astype(BF16)
        scores = lax.dot_general(c_ref[...], b_ref[...], (((1,), (1,)), ((), ())), preferred_element_type=F32)
        sm_ref[...] = jnp.where(row >= col, scores, 0.0)
        bt_ref[...] = b_ref[...].astype(F32).T.astype(BF16)

    width = x_ref.shape[1]
    row = lax.broadcasted_iota(jnp.int32, (HEADS, width), 0)
    col = lax.broadcasted_iota(jnp.int32, (HEADS, width), 1)
    spread = (row == step * (width // HDIM) + col // HDIM).astype(BF16)
    gain = jnp.dot(g_ref[...], spread, preferred_element_type=F32)
    scaled = (x_ref[...].astype(F32) * gain).astype(BF16)
    state = jnp.dot(bt_ref[...], scaled, preferred_element_type=F32).astype(BF16)
    for p in range(width // 128):
        l_ref[p] = state[:, 128 * p : 128 * (p + 1)]


def state_call(x, b, c, dt, bias, alog):
    steps = 8
    width = HEADS * HDIM // steps
    whole = lambda shape: pl.BlockSpec(shape, lambda i: (0,) * len(shape))
    return pl.pallas_call(
        state_kernel,
        grid=(steps,),
        in_specs=[
            pl.BlockSpec((TOK, width), lambda i: (0, i)),
            whole((TOK, DSTATE)),
            whole((TOK, DSTATE)),
            whole((TOK, HEADS)),
            whole((1, HEADS)),
            whole((1, HEADS)),
        ],
        out_specs=[
            pl.BlockSpec((width // 128, DSTATE, 128), lambda i: (i, 0, 0)),
            whole((TOK, HEADS)),
            whole((HEADS, TOK)),
            whole((TOK, TOK)),
        ],
        out_shape=[
            jax.ShapeDtypeStruct((PIECES, DSTATE, 128), BF16),
            jax.ShapeDtypeStruct((TOK, HEADS), F32),
            jax.ShapeDtypeStruct((HEADS, TOK), F32),
            jax.ShapeDtypeStruct((TOK, TOK), F32),
        ],
        scratch_shapes=[pltpu.VMEM((TOK, HEADS), BF16), pltpu.VMEM((DSTATE, TOK), BF16)],
        compiler_params=pltpu.CompilerParams(vmem_limit_bytes=VMEM_LIMIT),
        name="local_state",
    )(x, b, c, dt, bias, alog)


def scan_kernel(l_ref, d_ref, e_ref):
    def body(s, run):
        e_ref[s] = run.astype(BF16)
        return d_ref[pl.ds(s, 1), :] * run + l_ref[s].astype(F32)

    lax.fori_loop(0, l_ref.shape[0], body, jnp.zeros(l_ref.shape[1:], F32), unroll=4)


def out_kernel(x_ref, e_ref, c_ref, a_ref, rt_ref, sm_ref, skip_ref, o_ref):
    step = pl.program_id(0)
    pieces = x_ref.shape[1] // 128
    lane = lax.broadcasted_iota(jnp.int32, (TOK, 128), 1)
    first = lane < HDIM

    def body(p, carry):
        head = (step * pieces + p) * 2
        at = pl.ds(pl.multiple_of(p * 128, 128), 128)
        x = x_ref[:, at]
        turned = pltpu.roll(a_ref[...], lax.rem(HEADS - head, HEADS), 1)
        columns, parts = [], []
        for k in range(2):
            column = jnp.broadcast_to(turned[:, k : k + 1], (TOK, 128))
            columns.append(column)
            r = rt_ref[pl.ds(head + k, 1), :]
            rows = []
            for t0, t1 in ((0, 128), (128, 256), (256, TOK)):
                tiles = []
                for s0 in range(0, t1, 128):
                    s1 = min(s0 + 128, t1)
                    gap = column[t0:t1, : s1 - s0] - r[:, s0:s1]
                    if s1 > t0:
                        gap = jnp.minimum(gap, 100.0)
                    tiles.append((sm_ref[t0:t1, s0:s1] * jnp.exp2(gap)).astype(BF16))
                w = jnp.concatenate(tiles, axis=1) if len(tiles) > 1 else tiles[0]
                rows.append(jnp.dot(w, x[:t1], preferred_element_type=F32))
            parts.append(jnp.concatenate(rows, axis=0))
        within = jnp.where(first, parts[0], parts[1])
        fade = jnp.exp2(jnp.where(first, columns[0], columns[1]))
        carried = jnp.dot(c_ref[...], e_ref[p], preferred_element_type=F32)
        skip = jnp.where(first, skip_ref[0, head], skip_ref[0, head + 1])
        o_ref[:, at] = (within + carried * fade + skip * x.astype(F32)).astype(BF16)
        return carry

    lax.fori_loop(0, pieces, body, 0)


def out_call(x, e, c, a, rt, sm, skip):
    steps = 8
    width = HEADS * HDIM // steps
    whole = lambda shape: pl.BlockSpec(shape, lambda i: (0,) * len(shape))
    return pl.pallas_call(
        out_kernel,
        grid=(steps,),
        in_specs=[
            pl.BlockSpec((TOK, width), lambda i: (0, i)),
            pl.BlockSpec((width // 128, DSTATE, 128), lambda i: (i, 0, 0)),
            whole((TOK, DSTATE)),
            whole((TOK, HEADS)),
            whole((HEADS, TOK)),
            whole((TOK, TOK)),
            pl.BlockSpec(memory_space=pltpu.SMEM),
        ],
        out_specs=pl.BlockSpec((TOK, width), lambda i: (0, i)),
        out_shape=jax.ShapeDtypeStruct((TOK, HEADS * HDIM), BF16),
        compiler_params=pltpu.CompilerParams(vmem_limit_bytes=VMEM_LIMIT),
        name="outputs",
    )(x, e, c, a, rt, sm, skip)


def on_device(inputs, b_panel, c_panel, dt_raw, dt_bias, a_log, d_skip):
    axes = ("seq", "head")
    n = lax.axis_size(axes)
    states, a, rt, sm = state_call(inputs, b_panel, c_panel, dt_raw, dt_bias[None], a_log[None])
    share = PIECES * DSTATE // n
    ends = lax.all_gather(a[TOK - 1], axes, axis=0)
    mine = lax.all_to_all(states.reshape(n, share, 128), axes, 0, 0, tiled=True)
    here = lax.axis_index("seq") * lax.axis_size("head") + lax.axis_index("head")
    piece = here * share // DSTATE
    decay = jnp.repeat(jnp.exp2(lax.dynamic_slice_in_dim(ends, 2 * piece, 2, 1)), HDIM, axis=1)
    entering = pl.pallas_call(
        scan_kernel,
        out_shape=jax.ShapeDtypeStruct(mine.shape, BF16),
        compiler_params=pltpu.CompilerParams(vmem_limit_bytes=VMEM_LIMIT),
        name="scan_devices",
    )(mine, decay)
    entering = lax.all_to_all(entering, axes, 0, 0, tiled=True).reshape(PIECES, DSTATE, 128)
    return out_call(inputs, entering, c_panel, a, rt, sm, d_skip[None])


def solution(mesh):
    return jax.shard_map(
        on_device,
        mesh=mesh,
        in_specs=(P(("seq", "head"), None),) * 4 + (P(), P(), P()),
        out_specs=P(("seq", "head"), None),
        check_vma=False,
    )
```

time: 614 us -> 219 us (0.36)
  waiting for transfers between devices: 194 us -> 0.01 us
  local copies, waits for them, and re-layouts: 82.6 us -> 2.83 us
  other arithmetic: 75.7 us -> 0.35 us
  matrix products: 62.4 us -> 0 us
  Pallas kernels: 0 us -> 42.7 us
  blocking collectives: 121 us -> 157 us
  starting transfers between devices: 51.6 us -> 15.7 us
  between operations: 13.7 us -> 0.05 us
  loops' own time: 7.91 us -> 0 us
    all_gather x2 -> x0, waiting for transfers between devices: 166 us -> none  [the longest x1 90.1 us: on_device(): lax.all_gather(b_panel, 'head', axis=0, tiled=True)]
    all_gather x0 -> x1, blocking collectives: none -> 93.5 us  [on_device(): ends = lax.all_gather(a[TOK - 1], axes, axis=0)]
    dot_general x10 -> x0, matrix products: 62.4 us -> none  [the longest x4 27.3 us: head_terms(): jnp.einsum('kts,ksp->ktp', weights, tokens_head, preferred_element_type=j...]
    all_to_all x1, blocking collectives: 121 us -> 63.3 us  [on_device(): lax.all_to_all(entering, axes, 0, 0, tiled=True)]
    all_to_all x6 -> x0, local copies, waits for them, and re-layouts: 48.9 us -> none  [the longest x3 34.1 us: on_device(): lax.all_to_all(result, 'head', split_axis=0, concat_axis=1, tiled=True)]
    pallas_call x0 -> x3, Pallas kernels: none -> 42.7 us  [the longest x1 29.9 us: out_call(): pl.pallas_call(out_kernel, grid=(steps,), in_specs=[pl.BlockSpec((TOK, wi...]
    add x47 -> x0, other arithmetic: 42.4 us -> none  [the longest x40 41.8 us: advance(): factor[:, None, None] * state_now + update]
    ppermute x7 -> x0, starting transfers between devices: 33.7 us -> none  [passed_along(): return lax.ppermute(block, axis, route)]
  transfers between devices with their start and end apart: 11 -> 1, of which waited for: 10 -> 0; matrix products, arithmetic and copies ran while one was open for 3% -> 1% of each run, Pallas kernels for 0% -> 0%
where the time goes in v1:
time: 219 us; the launch traced here: 218 us
  blocking collectives  157 us (72%)
  Pallas kernels  42.7 us (19%)
  starting transfers between devices  15.7 us (7%)
  local copies, waits for them, and re-layouts  2.83 us (1%)
    all_gather x1, blocking collectives, on_device(): ends = lax.all_gather(a[TOK - 1], axes, axis=0)  93.5 us
    all_to_all x1, blocking collectives, on_device(): lax.all_to_all(entering, axes, 0, 0, tiled=True)  63.3 us
    pallas_call x1, Pallas kernels, out_call(): pl.pallas_call(out_kernel, grid=(steps,), in_specs=[pl.BlockSpec((TOK, wi...  29.9 us
    all_to_all x1, starting transfers between devices, on_device(): mine = lax.all_to_all(states.reshape(n, share, 128), axes, 0, 0, tiled=True)  15.7 us
    pallas_call x1, Pallas kernels, state_call(): pl.pallas_call(state_kernel, grid=(steps,), in_specs=[pl.BlockSpec((TOK,...  9.12 us
  transfers between devices with their start and end apart: 1, of which 0 were waited for; matrix products, arithmetic and copies ran while one was open for 1% of the time, Pallas kernels for 0%

profile of v1, /device:TPU:1, one launch (start us, length us, event | category | flops | bytes accessed | tf_op | source)
XLA Modules:
  0.0 218.4 jit_solution(15209833518017049420)
XLA Ops:
  0.0 9.1 %local_state.1 = (bf16[64,128,128]{2,1,0:T(8,128)(2,1)}, f32[320,128]{1,0:T(8,128)}, f32[128,320]{1,0:T(8,128)}, f32[320,320]{1,0:T(8,128)}) custom-call(bf16[320,8192]{1,0:T(8,128)(2,1)} %x_ref.3, bf16[320,128]{1,0:T(8,128)(2,1)} %b_ref.1, bf16[320,128]{1,0:T(8,128)(2,1)} %c_ref.3, bf16[320,128]{1,0:T(8,128)(2,1)} %dt_ref.1, f32[1,128]{1,0:T(1,128)} %bitcast.13, ...), custom_call_target="tpu_custom_call" | custom-call | tf_op jit(solution)/shard_map/local_state/pallas_call | solution.py:56
  9.1 15.7 %all-to-all-start = ((bf16[256,32,128]{2,1,0:T(8,128)(2,1)}), bf16[256,32,128]{2,1,0:T(8,128)(2,1)S(1)}, u32[]{:S(2)}, u32[]{:S(2)}) async-start(bf16[256,32,128]{2,1,0:T(8,128)(2,1)} %bitcast.10), calls=%async_computation | async-start | bytes 4194304 | tf_op jit(solution)/shard_map/all_to_all | solution.py:160
  24.8 0.7 slice_bitcast_fusion
  25.5 93.5 %all-gather = f32[256,1,128]{2,1,0:T(1,128)S(1)} all-gather(f32[1,1,128]{2,1,0:T(1,128)S(1)} %slice_bitcast_fusion), channel_id=1, replica_groups=mesh['seq'=8,'head'=32] {'seq','head'}, dimensions={0}, use_global_device_ids=true | all-gather | bytes 131584 | tf_op jit(solution)/shard_map/all_gather | solution.py:159
  119.0 0.3 multiply_exponential_fusion
  119.3 0.1 copy.10
  119.4 0.7 copy.11.d_ref
  120.2 0.0 all-to-all-done.l_ref
  120.2 0.0 copy-start
  120.2 1.3 copy-done
  121.5 3.6 %scan_devices.1 = bf16[256,32,128]{2,1,0:T(8,128)(2,1)} custom-call(bf16[256,32,128]{2,1,0:T(8,128)(2,1)} %copy-done, f32[256,128]{1,0:T(8,128)} %copy.11.d_ref), custom_call_target="tpu_custom_call" | custom-call | tf_op jit(solution)/shard_map/scan_devices/pallas_call | solution.py:164
  125.1 63.3 %all_to_all.10 = bf16[256,32,128]{2,1,0:T(8,128)(2,1)} all-to-all(bf16[256,32,128]{2,1,0:T(8,128)(2,1)} %scan_devices.1), channel_id=1, replica_groups=mesh['seq'=8,'head'=32] {'seq','head'}, dimensions={0} | all-to-all | bytes 4194304 | tf_op jit(solution)/shard_map/all_to_all | solution.py:170
  188.5 29.9 %outputs.1 = bf16[320,8192]{1,0:T(8,128)(2,1)} custom-call(bf16[320,8192]{1,0:T(8,128)(2,1)} %x_ref.3, bf16[64,128,128]{2,1,0:T(8,128)(2,1)} %bitcast.9, bf16[320,128]{1,0:T(8,128)(2,1)} %c_ref.3, f32[320,128]{1,0:T(8,128)} %get-tuple-element.10.a_ref, f32[128,320]{1,0:T(8,128)} %get-tuple-element.11.rt_ref, f32[320,320]{1,0:T(8,128)} %get-tuple-element.12.sm_ref, ...), custom_call_target="tpu_custom_call" | custom-call | tf_op jit(solution)/shard_map/outputs/pallas_call | solution.py:135
  (1 shorter events, 0.0 us)
Async XLA Ops:
  9.1 111.1 %all-to-all-start = ((bf16[256,32,128]{2,1,0:T(8,128)(2,1)}), bf16[256,32,128]{2,1,0:T(8,128)(2,1)S(1)}, u32[]{:S(2)}, u32[]{:S(2)}) async-start(bf16[256,32,128]{2,1,0:T(8,128)(2,1)} %bitcast.10), calls=%async_computation | async-start | bytes 4194304 | tf_op jit(solution)/shard_map/all_to_all | solution.py:160
  120.2 1.3 copy-start

commit v2 on v1

--- a/solution.py
+++ b/solution.py
@@ -82,12 +82,239 @@
     )(x, b, c, dt, bias, alog)
 
 
-def scan_kernel(l_ref, d_ref, e_ref):
-    def body(s, run):
-        e_ref[s] = run.astype(BF16)
-        return d_ref[pl.ds(s, 1), :] * run + l_ref[s].astype(F32)
-
-    lax.fori_loop(0, l_ref.shape[0], body, jnp.zeros(l_ref.shape[1:], F32), unroll=4)
+def link_kernel(cfg, l_ref, a_ref, fl, fr, fe, sl, sr, rs, rbuf, eb, za, pa, dec_own, dec_pre, dec_suf, rowdec,
+                fl_sem, fr_sem, fe_sem, left_sem, right_sem, rs_sem, rbuf_sem, eb_sem, z_send, z_recv, p_send, p_recv):
+    Z, Y, R, K, A, B, C = cfg
+    low = Z // 2 - 1
+    seq = lax.axis_index("seq")
+    head = lax.axis_index("head")
+    y = head // Z
+    z = head - y * Z
+    r = seq * Y + y
+    in_plane = (z == low) | (z == low + 1)
+    scan_piece = 2 * r + (z - low)
+
+    def remote(src, dst, send, recv, to_seq, to_head):
+        return pltpu.make_async_remote_copy(
+            src_ref=src, dst_ref=dst, send_sem=send, recv_sem=recv,
+            device_id={"seq": to_seq, "head": to_head}, device_id_type=pl.DeviceIdType.MESH,
+        )
+
+    def await_bytes(ref, sem):
+        pltpu.make_async_copy(ref, ref, sem).wait()
+
+    def send_left(src, q):
+        remote(src, fr.at[q], left_sem, fr_sem.at[q], seq, head - 1).start()
+
+    def send_right(src, q):
+        remote(src, fl.at[q], right_sem, fl_sem.at[q], seq, head + 1).start()
+
+    za[pl.ds(pl.multiple_of(z * 8, 8), 8), :] = jnp.broadcast_to(a_ref[TOK - 1 : TOK, :], (8, 128))
+    mine = za.at[pl.ds(pl.multiple_of(z * 8, 8), 8), :]
+    for dz in range(1, Z):
+        remote(mine, mine, z_send, z_recv, seq, y * Z + lax.rem(z + dz, Z)).start()
+    await_bytes(za.at[0 : 8 * (Z - 1), :], z_recv)
+    own = za[pl.ds(pl.multiple_of(z * 8, 8), 8), :]
+    before = jnp.zeros((8, 128), F32)
+    after = jnp.zeros((8, 128), F32)
+    for other in range(Z):
+        value = za[8 * other : 8 * other + 8, :]
+        before = before + jnp.where(other < z, value, 0.0)
+        after = after + jnp.where(other > z, value, 0.0)
+
+    @pl.when(in_plane)
+    def _():
+        slot = pl.ds(pl.multiple_of(r * 8, 8), 8)
+        pa[slot, :] = before + own + after
+
+        def tell(d, carry):
+            to = lax.rem(r + d, R)
+            to_seq = to // Y
+            remote(pa.at[slot, :], pa.at[slot, :], p_send, p_recv, to_seq, (to - to_seq * Y) * Z + z).start()
+            return carry
+
+        lax.fori_loop(1, R, tell, 0)
+
+    piece_at = lax.broadcasted_iota(jnp.int32, (K, 128), 0)
+    head_at = lax.broadcasted_iota(jnp.int32, (K, 128), 1)
+    pick_head = lax.broadcasted_iota(jnp.int32, (128, 128), 0)
+    pick_lane = lax.broadcasted_iota(jnp.int32, (128, 128), 1) // HDIM
+    second = (lax.rem(pick_head, 2) == pick_lane).astype(F32)
+    for value, out in ((own, dec_own), (before, dec_pre), (after, dec_suf)):
+        only = jnp.where(head_at // 2 == piece_at, value[0:1, :], 0.0)
+        logs = jnp.dot(only, second, precision=lax.Precision.HIGHEST, preferred_element_type=F32)
+        out[...] = jnp.exp2(logs)
+
+    def tick(i, carry):
+        for par in range(2):
+            m = low + par
+            q = i - (4 * A + B + C) - A * jnp.abs(z - m)
+            at = jnp.clip(q, 0, K - 1)
+            k = at // 2
+            valid = (q >= 0) & (q < K) & (lax.rem(at, 2) == par)
+
+            @pl.when(valid & (z < m))
+            def _():
+                remote(sl.at[at], fr.at[at], left_sem, fr_sem.at[at], seq, head + 1).wait_recv()
+
+                @pl.when(z > 0)
+                def _():
+                    send_left(fr.at[at], at)
+                    fl[at] = (fl[at].astype(F32) + dec_pre[pl.ds(at, 1), :] * fr[at].astype(F32)).astype(BF16)
+
+                @pl.when(z == 0)
+                def _():
+                    fl[at] = fr[at]
+
+            @pl.when(valid & (z == m))
+            def _():
+                @pl.when(k != r)
+                def _():
+                    to = lax.rem(r + 1, R)
+                    to_seq = to // Y
+                    remote(fe.at[k], fe.at[k], eb_sem, fe_sem.at[k], to_seq, (to - to_seq * Y) * Z + z).wait_recv()
+
+                send_left(fe.at[k], at)
+                entering = fl[at].astype(F32) + dec_pre[pl.ds(at, 1), :] * fe[k].astype(F32)
+                fl[at] = entering.astype(BF16)
+                sr[at] = (dec_own[pl.ds(at, 1), :] * entering + l_ref[at].astype(F32)).astype(BF16)
+                send_right(sr.at[at], at)
+
+            @pl.when(valid & (z > m))
+            def _():
+                remote(sr.at[at], fl.at[at], right_sem, fl_sem.at[at], seq, head - 1).wait_recv()
+
+                @pl.when(z < Z - 1)
+                def _():
+                    sr[at] = (dec_own[pl.ds(at, 1), :] * fl[at].astype(F32) + l_ref[at].astype(F32)).astype(BF16)
+                    send_right(sr.at[at], at)
+
+        q = i - A * z
+        at = jnp.clip(q, 0, K - 1)
+        valid = (q >= 0) & (q < K) & (z < low + lax.rem(at, 2))
+
+        @pl.when(valid & (z == 0))
+        def _():
+            send_right(l_ref.at[at], at)
+
+        @pl.when(valid & (z > 0))
+        def _():
+            remote(sr.at[at], fl.at[at], right_sem, fl_sem.at[at], seq, head - 1).wait_recv()
+            sr[at] = (dec_own[pl.ds(at, 1), :] * fl[at].astype(F32) + l_ref[at].astype(F32)).astype(BF16)
+            send_right(sr.at[at], at)
+
+        q1 = i - A * (Z - 1 - z)
+        at1 = jnp.clip(q1, 0, K - 1)
+        valid1 = (q1 >= 0) & (q1 < K) & (z > low + lax.rem(at1, 2))
+
+        @pl.when(valid1 & (z == Z - 1))
+        def _():
+            send_left(l_ref.at[at1], at1)
+
+        @pl.when(valid1 & (z < Z - 1))
+        def _():
+            remote(sl.at[at1], fr.at[at1], left_sem, fr_sem.at[at1], seq, head + 1).wait_recv()
+            sl[at1] = (dec_suf[pl.ds(at1, 1), :] * l_ref[at1].astype(F32) + fr[at1].astype(F32)).astype(BF16)
+            send_left(sl.at[at1], at1)
+
+        q2 = i - 4 * A
+        at2 = jnp.clip(q2, 0, K - 1)
+        k2 = at2 // 2
+
+        @pl.when((q2 >= 0) & (q2 < K) & (z == low + lax.rem(at2, 2)))
+        def _():
+            remote(sr.at[at2], fl.at[at2], right_sem, fl_sem.at[at2], seq, head - 1).wait_recv()
+            remote(sl.at[at2], fr.at[at2], left_sem, fr_sem.at[at2], seq, head + 1).wait_recv()
+            inner = dec_own[pl.ds(at2, 1), :] * fl[at2].astype(F32) + l_ref[at2].astype(F32)
+            total = (dec_suf[pl.ds(at2, 1), :] * inner + fr[at2].astype(F32)).astype(BF16)
+
+            @pl.when(k2 == r)
+            def _():
+                rbuf[r] = total
+
+            @pl.when(k2 != r)
+            def _():
+                rs[k2] = total
+                to_seq = k2 // Y
+                remote(rs.at[k2], rbuf.at[r], rs_sem, rbuf_sem, to_seq, (k2 - to_seq * Y) * Z + z).start()
+
+        @pl.when(in_plane & (i == scan_piece + 4 * A + B))
+        def _():
+            await_bytes(pa.at[0 : 8 * (R - 1), :], p_recv)
+            chosen = (pick_head == 2 * scan_piece + pick_lane).astype(F32)
+            rowdec[...] = jnp.exp2(
+                jnp.dot(pa[...], chosen, precision=lax.Precision.HIGHEST, preferred_element_type=F32)
+            )
+            await_bytes(rbuf.at[0 : R - 1], rbuf_sem)
+
+            def row(s, run):
+                e = run.astype(BF16)
+
+                @pl.when(s == r)
+                def _():
+                    fe[r] = e
+
+                @pl.when(s != r)
+                def _():
+                    eb[s] = e
+                    to_seq = s // Y
+                    remote(eb.at[s], fe.at[r], eb_sem, fe_sem.at[r], to_seq, (s - to_seq * Y) * Z + z).start()
+
+                return rowdec[pl.ds(s * 8, 1), :] * run + rbuf[s].astype(F32)
+
+            lax.fori_loop(0, R, row, jnp.zeros((DSTATE, 128), F32))
+
+        return carry
+
+    lax.fori_loop(0, K + 4 * A + B + C + A * (Z // 2), tick, 0)
+
+    await_bytes(za.at[0 : 8 * (Z - 1), :], z_send)
+
+    @pl.when(z > 0)
+    def _():
+        await_bytes(sl, left_sem)
+
+    @pl.when(z < Z - 1)
+    def _():
+        await_bytes(sr, right_sem)
+
+    @pl.when(in_plane)
+    def _():
+        await_bytes(pa.at[0 : 8 * (R - 1), :], p_send)
+        await_bytes(rbuf.at[0 : R - 1], rs_sem)
+        await_bytes(rbuf.at[0 : R - 1], eb_sem)
+
+
+def link_call(states, a, Z=8, K=PIECES, A=3, B=6, C=6):
+    Y = lax.axis_size("head") // Z
+    R = lax.axis_size("seq") * Y
+    tile = (DSTATE, 128)
+    dma = pltpu.SemaphoreType.DMA
+    return pl.pallas_call(
+        functools.partial(link_kernel, (Z, Y, R, K, A, B, C)),
+        in_specs=[pl.BlockSpec(memory_space=pltpu.VMEM)] * 2,
+        out_specs=pl.BlockSpec(memory_space=pltpu.VMEM),
+        out_shape=jax.ShapeDtypeStruct((K, *tile), BF16),
+        scratch_shapes=[
+            pltpu.VMEM((K, *tile), BF16),
+            pltpu.VMEM((K // 2, *tile), BF16),
+            pltpu.VMEM((K, *tile), BF16),
+            pltpu.VMEM((K, *tile), BF16),
+            pltpu.VMEM((K // 2, *tile), BF16),
+            pltpu.VMEM((R, *tile), BF16),
+            pltpu.VMEM((R, *tile), BF16),
+            pltpu.VMEM((Z * 8, 128), F32),
+            pltpu.VMEM((R * 8, 128), F32),
+            pltpu.VMEM((K, 128), F32),
+            pltpu.VMEM((K, 128), F32),
+            pltpu.VMEM((K, 128), F32),
+            pltpu.VMEM((R * 8, 128), F32),
+            dma((K,)), dma((K,)), dma((K // 2,)),
+            dma, dma, dma, dma, dma, dma, dma, dma, dma,
+        ],
+        compiler_params=pltpu.CompilerParams(vmem_limit_bytes=VMEM_LIMIT, has_side_effects=True),
+        name="link_states",
+    )(states, a)
 
 
 def out_kernel(x_ref, e_ref, c_ref, a_ref, rt_ref, sm_ref, skip_ref, o_ref):
@@ -152,22 +379,8 @@
 
 
 def on_device(inputs, b_panel, c_panel, dt_raw, dt_bias, a_log, d_skip):
-    axes = ("seq", "head")
-    n = lax.axis_size(axes)
     states, a, rt, sm = state_call(inputs, b_panel, c_panel, dt_raw, dt_bias[None], a_log[None])
-    share = PIECES * DSTATE // n
-    ends = lax.all_gather(a[TOK - 1], axes, axis=0)
-    mine = lax.all_to_all(states.reshape(n, share, 128), axes, 0, 0, tiled=True)
-    here = lax.axis_index("seq") * lax.axis_size("head") + lax.axis_index("head")
-    piece = here * share // DSTATE
-    decay = jnp.repeat(jnp.exp2(lax.dynamic_slice_in_dim(ends, 2 * piece, 2, 1)), HDIM, axis=1)
-    entering = pl.pallas_call(
-        scan_kernel,
-        out_shape=jax.ShapeDtypeStruct(mine.shape, BF16),
-        compiler_params=pltpu.CompilerParams(vmem_limit_bytes=VMEM_LIMIT),
-        name="scan_devices",
-    )(mine, decay)
-    entering = lax.all_to_all(entering, axes, 0, 0, tiled=True).reshape(PIECES, DSTATE, 128)
+    entering = link_call(states, a)
     return out_call(inputs, entering, c_panel, a, rt, sm, d_skip[None])
 
 

time: 219 us -> 184 us (0.84)
  blocking collectives: 157 us -> 0 us
  Pallas kernels: 42.7 us -> 182 us
  starting transfers between devices: 15.7 us -> 0 us
  local copies, waits for them, and re-layouts: 2.83 us -> 0 us
    pallas_call x1, Pallas kernels: 3.61 us -> 143 us  [link_call(): pl.pallas_call(functools.partial(link_kernel, (Z, Y, R, K, A, B, C)), in_...]
    all_gather x1 -> x0, blocking collectives: 93.5 us -> none  [on_device(): ends = lax.all_gather(a[TOK - 1], axes, axis=0)]
    all_to_all x1 -> x0, blocking collectives: 63.3 us -> none  [on_device(): lax.all_to_all(entering, axes, 0, 0, tiled=True)]
    all_to_all x1 -> x0, starting transfers between devices: 15.7 us -> none  [on_device(): mine = lax.all_to_all(states.reshape(n, share, 128), axes, 0, 0, tiled=True)]
  transfers between devices with their start and end apart: 1 -> 0, of which waited for: 0 -> 0; matrix products, arithmetic and copies ran while one was open for 1% -> 0% of each run, Pallas kernels for 0% -> 0%
where the time goes in v2:
time: 184 us; the launch traced here: 182 us
  Pallas kernels  182 us (99%)
    pallas_call x1, Pallas kernels, link_call(): pl.pallas_call(functools.partial(link_kernel, (Z, Y, R, K, A, B, C)), in_...  143 us
    pallas_call x1, Pallas kernels, out_call(): pl.pallas_call(out_kernel, grid=(steps,), in_specs=[pl.BlockSpec((TOK, wi...  30 us
    pallas_call x1, Pallas kernels, state_call(): pl.pallas_call(state_kernel, grid=(steps,), in_specs=[pl.BlockSpec((TOK,...  9.12 us

profile of v2, /device:TPU:1, one launch (start us, length us, event | category | flops | bytes accessed | tf_op | source)
XLA Modules:
  0.0 181.7 jit_solution(8662699887333741265)
XLA Ops:
  0.0 9.1 %local_state.1 = (bf16[64,128,128]{2,1,0:T(8,128)(2,1)}, f32[320,128]{1,0:T(8,128)}, f32[128,320]{1,0:T(8,128)}, f32[320,320]{1,0:T(8,128)}) custom-call(bf16[320,8192]{1,0:T(8,128)(2,1)} %x_ref.3, bf16[320,128]{1,0:T(8,128)(2,1)} %b_ref.1, bf16[320,128]{1,0:T(8,128)(2,1)} %c_ref.3, bf16[320,128]{1,0:T(8,128)(2,1)} %dt_ref.1, f32[1,128]{1,0:T(1,128)} %bitcast.3, ...), custom_call_target="tpu_custom_call" | custom-call | tf_op jit(solution)/shard_map/local_state/pallas_call | solution.py:56
  9.1 142.6 %link_states.1.e_ref = bf16[64,128,128]{2,1,0:T(8,128)(2,1)} custom-call(bf16[64,128,128]{2,1,0:T(8,128)(2,1)} %get-tuple-element.9.l_ref, f32[320,128]{1,0:T(8,128)} %get-tuple-element.10.a_ref), custom_call_target="tpu_custom_call" | custom-call | tf_op jit(solution)/shard_map/link_states/pallas_call | solution.py:293
  151.7 30.0 %outputs.1 = bf16[320,8192]{1,0:T(8,128)(2,1)} custom-call(bf16[320,8192]{1,0:T(8,128)(2,1)} %x_ref.3, bf16[64,128,128]{2,1,0:T(8,128)(2,1)} %link_states.1.e_ref, bf16[320,128]{1,0:T(8,128)(2,1)} %c_ref.3, f32[320,128]{1,0:T(8,128)} %get-tuple-element.10.a_ref, f32[128,320]{1,0:T(8,128)} %get-tuple-element.11.rt_ref, f32[320,320]{1,0:T(8,128)} %get-tuple-element.12.sm_ref, ...), custom_call_target="tpu_custom_call" | custom-call | tf_op jit(solution)/shard_map/outputs/pallas_call | solution.py:362

commit v3 on v2

v3 whole, which is shorter than its diff:
```python
import functools

import jax
import jax.numpy as jnp
from jax import lax
from jax.experimental import pallas as pl
from jax.experimental.pallas import tpu as pltpu
from jax.sharding import PartitionSpec as P

HEADS = 128
HDIM = 64
DSTATE = 128
TOK = 320
PIECES = HEADS // 2
PARTS = 4
TURNS = 4
XBLOCKS = 8
LOG2E = 1.4426950408889634
F32 = jnp.float32
BF16 = jnp.bfloat16
VMEM_LIMIT = 56 * 1024 * 1024


def layer_kernel(cfg, x_hbm, b_ref, c_ref, dt_ref, bias_ref, alog_ref, skip_ref, o_hbm,
                 x_ref, o_ref, part_ref, fade_ref, a_ref, rt_ref, sm_ref, g_ref, bt_ref,
                 l_ref, fl, fr, fe, sl, sr, rs, rbuf, eb, za, pa, dec_own, dec_pre, dec_suf, rowdec,
                 x_sem, o_sem, fl_sem, fr_sem, fe_sem, left_sem, right_sem, rs_sem, rbuf_sem, eb_sem,
                 z_send, z_recv, p_send, p_recv):
    Z, Y, R, K, A, B, C = cfg
    low = Z // 2 - 1
    seq = lax.axis_index("seq")
    head = lax.axis_index("head")
    y = head // Z
    z = head - y * Z
    r = seq * Y + y
    in_plane = (z == low) | (z == low + 1)
    part = lax.rem(r, PARTS)
    rows = DSTATE // PARTS

    def remote(src, dst, send, recv, to_seq, to_head):
        return pltpu.make_async_remote_copy(
            src_ref=src, dst_ref=dst, send_sem=send, recv_sem=recv,
            device_id={"seq": to_seq, "head": to_head}, device_id_type=pl.DeviceIdType.MESH,
        )

    def await_bytes(ref, sem):
        pltpu.make_async_copy(ref, ref, sem).wait()

    def send_left(src, q):
        remote(src, fr.at[q], left_sem, fr_sem.at[q], seq, head - 1).start()

    def send_right(src, q):
        remote(src, fl.at[q], right_sem, fl_sem.at[q], seq, head + 1).start()

    gate = pltpu.get_barrier_semaphore()

    def greet(to_seq, to_head):
        pl.semaphore_signal(
            gate, inc=1, device_id={"seq": to_seq, "head": to_head}, device_id_type=pl.DeviceIdType.MESH
        )

    for dz in range(1, Z):
        greet(seq, y * Z + lax.rem(z + dz, Z))

    @pl.when(in_plane)
    def _():
        def hello(d, carry):
            to = lax.rem(r + d, R)
            to_seq = to // Y
            greet(to_seq, (to - to_seq * Y) * Z + z)
            return carry

        lax.fori_loop(1, R, hello, 0)

    blocks = XBLOCKS
    width = K * 128 // blocks

    def x_copy(n):
        cols = pl.ds(pl.multiple_of(n * width, width), width)
        return pltpu.make_async_copy(x_hbm.at[:, cols], x_ref.at[:, cols], x_sem.at[n])

    for n in range(blocks):
        x_copy(n).start()

    v = dt_ref[...].astype(F32) + bias_ref[...]
    delta = jnp.maximum(v, 0.0) + jnp.log(1.0 + jnp.exp(-jnp.abs(v)))
    rates = (-LOG2E) * jnp.exp(alog_ref[...]) * delta
    t_at = lax.broadcasted_iota(jnp.int32, (TOK, TOK), 0)
    s_at = lax.broadcasted_iota(jnp.int32, (TOK, TOK), 1)
    lower = (t_at >= s_at).astype(F32)
    a = jnp.dot(lower, rates, precision=lax.Precision.HIGHEST, preferred_element_type=F32)
    a_ref[...] = a
    rt_ref[...] = (a - jnp.log2(delta)).T
    g_ref[...] = (jnp.exp2(a[TOK - 1 : TOK, :] - a) * delta).astype(BF16)
    scores = lax.dot_general(c_ref[...], b_ref[...], (((1,), (1,)), ((), ())), preferred_element_type=F32)
    sm_ref[...] = jnp.where(t_at >= s_at, scores, 0.0)
    bt_ref[...] = b_ref[...].astype(F32).T.astype(BF16)

    pl.semaphore_wait(gate, Z - 1 + jnp.where(in_plane, R - 1, 0))

    za[pl.ds(pl.multiple_of(z * 8, 8), 8), :] = jnp.broadcast_to(a_ref[TOK - 1 : TOK, :], (8, 128))
    mine = za.at[pl.ds(pl.multiple_of(z * 8, 8), 8), :]
    for dz in range(1, Z):
        remote(mine, mine, z_send, z_recv, seq, y * Z + lax.rem(z + dz, Z)).start()
    await_bytes(za.at[0 : 8 * (Z - 1), :], z_recv)
    own = za[pl.ds(pl.multiple_of(z * 8, 8), 8), :]
    before = jnp.zeros((8, 128), F32)
    after = jnp.zeros((8, 128), F32)
    for other in range(Z):
        value = za[8 * other : 8 * other + 8, :]
        before = before + jnp.where(other < z, value, 0.0)
        after = after + jnp.where(other > z, value, 0.0)

    @pl.when(in_plane)
    def _():
        slot = pl.ds(pl.multiple_of(r * 8, 8), 8)
        pa[slot, :] = before + own + after

        def tell(d, carry):
            to = lax.rem(r + d, R)
            to_seq = to // Y
            remote(pa.at[slot, :], pa.at[slot, :], p_send, p_recv, to_seq, (to - to_seq * Y) * Z + z).start()
            return carry

        lax.fori_loop(1, R, tell, 0)

    piece_at = lax.broadcasted_iota(jnp.int32, (K, 128), 0)
    head_at = lax.broadcasted_iota(jnp.int32, (K, 128), 1)
    pick_head = lax.broadcasted_iota(jnp.int32, (128, 128), 0)
    pick_lane = lax.broadcasted_iota(jnp.int32, (128, 128), 1) // HDIM
    second = (lax.rem(pick_head, 2) == pick_lane).astype(F32)
    for value, out in ((own, dec_own), (before, dec_pre), (after, dec_suf)):
        only = jnp.where(head_at // 2 == piece_at, value[0:1, :], 0.0)
        logs = jnp.dot(only, second, precision=lax.Precision.HIGHEST, preferred_element_type=F32)
        out[...] = jnp.exp2(logs)

    lane = lax.broadcasted_iota(jnp.int32, (TOK, 128), 1)
    first = lane < HDIM

    def columns_of(q):
        return pl.ds(pl.multiple_of(q * 128, 128), 128)

    def local_state(q):
        spread = (pick_head == 2 * q + pick_lane).astype(BF16)
        gain = jnp.dot(g_ref[...], spread, preferred_element_type=F32)
        scaled = (x_ref[:, columns_of(q)].astype(F32) * gain).astype(BF16)
        l_ref[q] = jnp.dot(bt_ref[...], scaled, preferred_element_type=F32).astype(BF16)

    def within_and_skip(q):
        x = x_ref[:, columns_of(q)]
        turned = pltpu.roll(a_ref[...], lax.rem(HEADS - 2 * q, HEADS), 1)
        columns, parts = [], []
        for k in range(2):
            column = jnp.broadcast_to(turned[:, k : k + 1], (TOK, 128))
            columns.append(column)
            row = rt_ref[pl.ds(2 * q + k, 1), :]
            outs = []
            for t0, t1 in ((0, 128), (128, 256), (256, TOK)):
                tiles = []
                for s0 in range(0, t1, 128):
                    s1 = min(s0 + 128, t1)
                    gap = column[t0:t1, : s1 - s0] - row[:, s0:s1]
                    if s1 > t0:
                        gap = jnp.minimum(gap, 100.0)
                    tiles.append((sm_ref[t0:t1, s0:s1] * jnp.exp2(gap)).astype(BF16))
                w = jnp.concatenate(tiles, axis=1) if len(tiles) > 1 else tiles[0]
                outs.append(jnp.dot(w, x[:t1], preferred_element_type=F32))
            parts.append(jnp.concatenate(outs, axis=0))
        fade_ref[q] = jnp.exp2(jnp.where(first, columns[0], columns[1]))
        skip = jnp.where(first, skip_ref[0, 2 * q], skip_ref[0, 2 * q + 1])
        part_ref[q] = jnp.where(first, parts[0], parts[1]) + skip * x.astype(F32)

    def finish(q):
        carried = jnp.dot(c_ref[...], fl[q], preferred_element_type=F32)
        o_ref[:, columns_of(q)] = (part_ref[q] + fade_ref[q] * carried).astype(BF16)
        pltpu.make_async_copy(o_ref.at[:, columns_of(q)], o_hbm.at[:, columns_of(q)], o_sem).start()

    def tick(i, carry):
        for par in range(2):
            m = low + par
            q = i - (4 * A + B + C) - A * jnp.abs(z - m)
            at = jnp.clip(q, 0, K - 1)
            k = at // 2
            valid = (q >= 0) & (q < K) & (lax.rem(at, 2) == par)

            @pl.when(valid & (z < m))
            def _():
                remote(sl.at[at], fr.at[at], left_sem, fr_sem.at[at], seq, head + 1).wait_recv()

                @pl.when(z > 0)
                def _():
                    send_left(fr.at[at], at)
                    fl[at] = (fl[at].astype(F32) + dec_pre[pl.ds(at, 1), :] * fr[at].astype(F32)).astype(BF16)

                @pl.when(z == 0)
                def _():
                    fl[at] = fr[at]

            @pl.when(valid & (z == m))
            def _():
                mine = r // PARTS == lax.rem(k, R // PARTS)

                @pl.when(mine)
                def _():
                    await_bytes(fe.at[k, 0 : rows * (PARTS - 1)], fe_sem.at[k])

                @pl.when(jnp.logical_not(mine))
                def _():
                    await_bytes(fe.at[k], fe_sem.at[k])

                send_left(fe.at[k], at)
                entering = fl[at].astype(F32) + dec_pre[pl.ds(at, 1), :] * fe[k].astype(F32)
                fl[at] = entering.astype(BF16)
                sr[at] = (dec_own[pl.ds(at, 1), :] * entering + l_ref[at].astype(F32)).astype(BF16)
                send_right(sr.at[at], at)

            @pl.when(valid & (z > m))
            def _():
                remote(sr.at[at], fl.at[at], right_sem, fl_sem.at[at], seq, head - 1).wait_recv()

                @pl.when(z < Z - 1)
                def _():
                    sr[at] = (dec_own[pl.ds(at, 1), :] * fl[at].astype(F32) + l_ref[at].astype(F32)).astype(BF16)
                    send_right(sr.at[at], at)

        ahead = jnp.minimum(i, K - 1)
        per_block = K // XBLOCKS

        @pl.when((i < K) & (lax.rem(ahead, per_block) == 0))
        def _():
            x_copy(ahead // per_block).wait()

        @pl.when(i < K)
        def _():
            local_state(ahead)

        q = i - A * z
        at = jnp.clip(q, 0, K - 1)
        valid = (q >= 0) & (q < K) & (z < low + lax.rem(at, 2))

        @pl.when(valid & (z == 0))
        def _():
            send_right(l_ref.at[at], at)

        @pl.when(valid & (z > 0))
        def _():
            remote(sr.at[at], fl.at[at], right_sem, fl_sem.at[at], seq, head - 1).wait_recv()
            sr[at] = (dec_own[pl.ds(at, 1), :] * fl[at].astype(F32) + l_ref[at].astype(F32)).astype(BF16)
            send_right(sr.at[at], at)

        q1 = i - A * (Z - 1 - z)
        at1 = jnp.clip(q1, 0, K - 1)
        valid1 = (q1 >= 0) & (q1 < K) & (z > low + lax.rem(at1, 2))

        @pl.when(valid1 & (z == Z - 1))
        def _():
            send_left(l_ref.at[at1], at1)

        @pl.when(valid1 & (z < Z - 1))
        def _():
            remote(sl.at[at1], fr.at[at1], left_sem, fr_sem.at[at1], seq, head + 1).wait_recv()
            sl[at1] = (dec_suf[pl.ds(at1, 1), :] * l_ref[at1].astype(F32) + fr[at1].astype(F32)).astype(BF16)
            send_left(sl.at[at1], at1)

        q2 = i - 4 * A
        at2 = jnp.clip(q2, 0, K - 1)
        k2 = at2 // 2

        @pl.when((q2 >= 0) & (q2 < K) & (z == low + lax.rem(at2, 2)))
        def _():
            remote(sr.at[at2], fl.at[at2], right_sem, fl_sem.at[at2], seq, head - 1).wait_recv()
            remote(sl.at[at2], fr.at[at2], left_sem, fr_sem.at[at2], seq, head + 1).wait_recv()
            inner = dec_own[pl.ds(at2, 1), :] * fl[at2].astype(F32) + l_ref[at2].astype(F32)
            total = (dec_suf[pl.ds(at2, 1), :] * inner + fr[at2].astype(F32)).astype(BF16)

            rs[k2] = total
            base = lax.rem(k2, R // PARTS) * PARTS
            turn = k2 // (R // PARTS)
            for p in range(PARTS):
                to = base + p

                @pl.when(to == r)
                def _():
                    rbuf[turn, r] = total[rows * p : rows * (p + 1)]

                @pl.when(to != r)
                def _():
                    to_seq = to // Y
                    remote(
                        rs.at[k2, rows * p : rows * (p + 1)], rbuf.at[turn, r], rs_sem, rbuf_sem.at[turn],
                        to_seq, (to - to_seq * Y) * Z + z,
                    ).start()

        @pl.when(in_plane & (i == 4 * A))
        def _():
            await_bytes(pa.at[0 : 8 * (R - 1), :], p_recv)

        for turn in range(TURNS):
            k3 = r // PARTS + turn * (R // PARTS)
            q3 = 2 * k3 + (z - low)

            @pl.when(in_plane & (i == q3 + 4 * A + B))
            def _():
                chosen = (pick_head == 2 * q3 + pick_lane).astype(F32)
                rowdec[...] = jnp.exp2(
                    jnp.dot(pa[...], chosen, precision=lax.Precision.HIGHEST, preferred_element_type=F32)
                )
                await_bytes(rbuf.at[turn, 0 : R - 1], rbuf_sem.at[turn])
                span = pl.ds(pl.multiple_of(part * rows, rows), rows)

                def row(s, run):
                    e = run.astype(BF16)

                    @pl.when(s == r)
                    def _():
                        fe[k3, span] = e

                    @pl.when(s != r)
                    def _():
                        eb[turn, s] = e
                        to_seq = s // Y
                        remote(
                            eb.at[turn, s], fe.at[k3, span], eb_sem, fe_sem.at[k3],
                            to_seq, (s - to_seq * Y) * Z + z,
                        ).start()

                    return rowdec[pl.ds(s * 8, 1), :] * run + rbuf[turn, s].astype(F32)

                lax.fori_loop(0, R, row, jnp.zeros((rows, 128), F32))

        w = i // 3 * 2 + lax.rem(i, 3)
        w_at = jnp.minimum(w, K - 1)

        @pl.when((lax.rem(i, 3) < 2) & (w < K))
        def _():
            within_and_skip(w_at)

        for par in range(2):
            q = i - (4 * A + B + C) - A * jnp.abs(z - low - par)
            at = jnp.clip(q, 0, K - 1)

            @pl.when((q >= 0) & (q < K) & (lax.rem(at, 2) == par))
            def _():
                finish(at)

        return carry

    lax.fori_loop(0, K + 4 * A + B + C + A * (Z // 2), tick, 0)

    pltpu.make_async_copy(o_ref, o_hbm, o_sem).wait()
    await_bytes(za.at[0 : 8 * (Z - 1), :], z_send)

    @pl.when(z > 0)
    def _():
        await_bytes(sl, left_sem)

    @pl.when(z < Z - 1)
    def _():
        await_bytes(sr, right_sem)

    @pl.when(in_plane)
    def _():
        await_bytes(pa.at[0 : 8 * (R - 1), :], p_send)
        for turn in range(TURNS):
            await_bytes(rbuf.at[turn, 0 : R - 1], rs_sem)
            await_bytes(rbuf.at[turn, 0 : R - 1], eb_sem)


def layer_call(x, b, c, dt, bias, alog, skip, Z=8, K=PIECES, A=6, B=8, C=10):
    Y = lax.axis_size("head") // Z
    R = lax.axis_size("seq") * Y
    tile = (DSTATE, 128)
    dma = pltpu.SemaphoreType.DMA
    vmem = pl.BlockSpec(memory_space=pltpu.VMEM)
    hbm = pl.BlockSpec(memory_space=pl.ANY)
    small = pltpu.VMEM((R * 8, 128), F32)
    share = pltpu.VMEM((TURNS, R, DSTATE // PARTS, 128), BF16)
    return pl.pallas_call(
        functools.partial(layer_kernel, (Z, Y, R, K, A, B, C)),
        in_specs=[hbm, vmem, vmem, vmem, vmem, vmem, pl.BlockSpec(memory_space=pltpu.SMEM)],
        out_specs=hbm,
        out_shape=jax.ShapeDtypeStruct((TOK, K * 128), BF16),
        scratch_shapes=[
            pltpu.VMEM((TOK, K * 128), BF16),
            pltpu.VMEM((TOK, K * 128), BF16),
            pltpu.VMEM((K, TOK, 128), F32),
            pltpu.VMEM((K, TOK, 128), F32),
            pltpu.VMEM((TOK, HEADS), F32),
            pltpu.VMEM((HEADS, TOK), F32),
            pltpu.VMEM((TOK, TOK), F32),
            pltpu.VMEM((TOK, HEADS), BF16),
            pltpu.VMEM((DSTATE, TOK), BF16),
            pltpu.VMEM((K, *tile), BF16),
            pltpu.VMEM((K, *tile), BF16),
            pltpu.VMEM((K, *tile), BF16),
            pltpu.VMEM((K // 2, *tile), BF16),
            pltpu.VMEM((K, *tile), BF16),
            pltpu.VMEM((K, *tile), BF16),
            pltpu.VMEM((K // 2, *tile), BF16),
            share,
            share,
            pltpu.VMEM((Z * 8, 128), F32),
            small,
            pltpu.VMEM((K, 128), F32),
            pltpu.VMEM((K, 128), F32),
            pltpu.VMEM((K, 128), F32),
            small,
            dma((XBLOCKS,)), dma, dma((K,)), dma((K,)), dma((K // 2,)),
            dma, dma, dma, dma((TURNS,)), dma, dma, dma, dma, dma,
        ],
        compiler_params=pltpu.CompilerParams(
            vmem_limit_bytes=VMEM_LIMIT, has_side_effects=True, collective_id=0
        ),
        name="layer",
    )(x, b, c, dt, bias, alog, skip)


def on_device(inputs, b_panel, c_panel, dt_raw, dt_bias, a_log, d_skip):
    return layer_call(inputs, b_panel, c_panel, dt_raw, dt_bias[None], a_log[None], d_skip[None])


def solution(mesh):
    return jax.shard_map(
        on_device,
        mesh=mesh,
        in_specs=(P(("seq", "head"), None),) * 4 + (P(), P(), P()),
        out_specs=P(("seq", "head"), None),
        check_vma=False,
    )
```

time: 184 us -> 123 us (0.67); the launches traced: 182 us -> 123 us
  Pallas kernels: 182 us -> 118 us
  local copies, waits for them, and re-layouts: 0 us -> 5.43 us
    pallas_call x3 -> x1, Pallas kernels: 182 us -> 118 us  [layer_call(): pl.pallas_call(functools.partial(layer_kernel, (Z, Y, R, K, A, B, C)), in...]
    unnamed x0 -> x1, local copies, waits for them, and re-layouts: none -> 5.43 us
where the time goes in v3:
time: 123 us
  Pallas kernels  118 us (96%)
  local copies, waits for them, and re-layouts  5.43 us (4%)
    pallas_call x1, Pallas kernels, layer_call(): pl.pallas_call(functools.partial(layer_kernel, (Z, Y, R, K, A, B, C)), in...  118 us
    unnamed x1, local copies, waits for them, and re-layouts  5.43 us

profile of v3, /device:TPU:1, one launch (start us, length us, event | category | flops | bytes accessed | tf_op | source)
XLA Modules:
  0.0 123.1 jit_solution(11765628466180653878)
XLA Ops:
  0.0 117.6 %layer.1 = bf16[320,8192]{1,0:T(8,128)(2,1)} custom-call(bf16[320,8192]{1,0:T(8,128)(2,1)} %x_hbm.1, bf16[320,128]{1,0:T(8,128)(2,1)} %b_ref.1, bf16[320,128]{1,0:T(8,128)(2,1)} %c_ref.1, bf16[320,128]{1,0:T(8,128)(2,1)} %dt_ref.1, f32[1,128]{1,0:T(1,128)} %bitcast.3, f32[1,128]{1,0:T(1,128)} %bitcast.4, f32[1,128]{1,0:T(1,128)} %bitcast.5), custom_call_target="tpu_custom_call" | custom-call | tf_op jit(solution)/shard_map/layer/pallas_call | solution.py:378
  117.6 5.4 %copy.9 = bf16[320,8192]{1,0:T(8,128)(2,1)} copy(bf16[320,8192]{1,0:T(8,128)(2,1)} %layer.1) | data formatting | bytes 10485760

commit v4 on v3

--- a/solution.py
+++ b/solution.py
@@ -15,18 +15,21 @@
 PARTS = 4
 TURNS = 4
 XBLOCKS = 8
+BATCH = 4
+FILL = 24
+MEET = 5
 LOG2E = 1.4426950408889634
 F32 = jnp.float32
 BF16 = jnp.bfloat16
 VMEM_LIMIT = 56 * 1024 * 1024
 
 
-def layer_kernel(cfg, x_hbm, b_ref, c_ref, dt_ref, bias_ref, alog_ref, skip_ref, o_hbm,
-                 x_ref, o_ref, part_ref, fade_ref, a_ref, rt_ref, sm_ref, g_ref, bt_ref,
+def layer_kernel(cfg, x_hbm, b_ref, c_ref, dt_ref, bias_ref, alog_ref, skip_ref, o_ref,
+                 x_ref, part_ref, fade_ref, a_ref, rt_ref, sm_ref, g_ref, bt_ref,
                  l_ref, fl, fr, fe, sl, sr, rs, rbuf, eb, za, pa, dec_own, dec_pre, dec_suf, rowdec,
-                 x_sem, o_sem, fl_sem, fr_sem, fe_sem, left_sem, right_sem, rs_sem, rbuf_sem, eb_sem,
+                 x_sem, fl_sem, fr_sem, fe_sem, left_sem, right_sem, rs_sem, rbuf_sem, eb_sem,
                  z_send, z_recv, p_send, p_recv):
-    Z, Y, R, K, A, B, C = cfg
+    Z, Y, R, K, A, AO, B, C = cfg
     low = Z // 2 - 1
     seq = lax.axis_index("seq")
     head = lax.axis_index("head")
@@ -34,8 +37,15 @@
     z = head - y * Z
     r = seq * Y + y
     in_plane = (z == low) | (z == low + 1)
-    part = lax.rem(r, PARTS)
+    groups = R // PARTS
+    part = r // groups
+    rest = lax.rem(r, groups)
+    diagonal = groups % Y == 0
+    group = rest // Y * Y + lax.rem(rest - part + PARTS * Y, Y) if diagonal else rest
     rows = DSTATE // PARTS
+
+    def owner(g, p):
+        return p * groups + (g // Y * Y + lax.rem(p + g, Y) if diagonal else g)
 
     def remote(src, dst, send, recv, to_seq, to_head):
         return pltpu.make_async_remote_copy(
@@ -90,49 +100,65 @@
     lower = (t_at >= s_at).astype(F32)
     a = jnp.dot(lower, rates, precision=lax.Precision.HIGHEST, preferred_element_type=F32)
     a_ref[...] = a
-    rt_ref[...] = (a - jnp.log2(delta)).T
     g_ref[...] = (jnp.exp2(a[TOK - 1 : TOK, :] - a) * delta).astype(BF16)
-    scores = lax.dot_general(c_ref[...], b_ref[...], (((1,), (1,)), ((), ())), preferred_element_type=F32)
-    sm_ref[...] = jnp.where(t_at >= s_at, scores, 0.0)
     bt_ref[...] = b_ref[...].astype(F32).T.astype(BF16)
-
-    pl.semaphore_wait(gate, Z - 1 + jnp.where(in_plane, R - 1, 0))
-
-    za[pl.ds(pl.multiple_of(z * 8, 8), 8), :] = jnp.broadcast_to(a_ref[TOK - 1 : TOK, :], (8, 128))
-    mine = za.at[pl.ds(pl.multiple_of(z * 8, 8), 8), :]
-    for dz in range(1, Z):
-        remote(mine, mine, z_send, z_recv, seq, y * Z + lax.rem(z + dz, Z)).start()
-    await_bytes(za.at[0 : 8 * (Z - 1), :], z_recv)
-    own = za[pl.ds(pl.multiple_of(z * 8, 8), 8), :]
-    before = jnp.zeros((8, 128), F32)
-    after = jnp.zeros((8, 128), F32)
-    for other in range(Z):
-        value = za[8 * other : 8 * other + 8, :]
-        before = before + jnp.where(other < z, value, 0.0)
-        after = after + jnp.where(other > z, value, 0.0)
-
-    @pl.when(in_plane)
-    def _():
-        slot = pl.ds(pl.multiple_of(r * 8, 8), 8)
-        pa[slot, :] = before + own + after
-
-        def tell(d, carry):
-            to = lax.rem(r + d, R)
-            to_seq = to // Y
-            remote(pa.at[slot, :], pa.at[slot, :], p_send, p_recv, to_seq, (to - to_seq * Y) * Z + z).start()
-            return carry
-
-        lax.fori_loop(1, R, tell, 0)
 
     piece_at = lax.broadcasted_iota(jnp.int32, (K, 128), 0)
     head_at = lax.broadcasted_iota(jnp.int32, (K, 128), 1)
     pick_head = lax.broadcasted_iota(jnp.int32, (128, 128), 0)
     pick_lane = lax.broadcasted_iota(jnp.int32, (128, 128), 1) // HDIM
-    second = (lax.rem(pick_head, 2) == pick_lane).astype(F32)
-    for value, out in ((own, dec_own), (before, dec_pre), (after, dec_suf)):
-        only = jnp.where(head_at // 2 == piece_at, value[0:1, :], 0.0)
+
+    def per_piece(value):
+        second = (lax.rem(pick_head, 2) == pick_lane).astype(F32)
+        only = jnp.where(head_at // 2 == piece_at, value, 0.0)
         logs = jnp.dot(only, second, precision=lax.Precision.HIGHEST, preferred_element_type=F32)
-        out[...] = jnp.exp2(logs)
+        return jnp.exp2(logs)
+
+    dec_own[...] = per_piece(a[TOK - 1 : TOK, :])
+    my_row = pl.ds(pl.multiple_of(z * 8, 8), 8)
+    za[my_row, :] = jnp.broadcast_to(a[TOK - 1 : TOK, :], (8, 128))
+
+    pl.semaphore_wait(gate, Z - 1 + jnp.where(in_plane, R - 1, 0))
+
+    for dz in range(1, Z):
+        remote(za.at[my_row, :], za.at[my_row, :], z_send, z_recv, seq, y * Z + lax.rem(z + dz, Z)).start()
+
+    def meet_row():
+        await_bytes(za.at[0 : 8 * (Z - 1), :], z_recv)
+        before = jnp.zeros((8, 128), F32)
+        after = jnp.zeros((8, 128), F32)
+        for other in range(Z):
+            value = za[8 * other : 8 * other + 8, :]
+            before = before + jnp.where(other < z, value, 0.0)
+            after = after + jnp.where(other > z, value, 0.0)
+        total = before + after + za[my_row, :]
+
+        @pl.when(in_plane)
+        def _():
+            slot = pl.ds(pl.multiple_of(r * 8, 8), 8)
+            pa[slot, :] = total
+
+            def tell(d, carry):
+                to = lax.rem(r + d, R)
+                to_seq = to // Y
+                remote(
+                    pa.at[slot, :], pa.at[slot, :], p_send, p_recv, to_seq, (to - to_seq * Y) * Z + z
+                ).start()
+                return carry
+
+            lax.fori_loop(1, R, tell, 0)
+
+        dec_pre[...] = per_piece(before[0:1, :])
+        dec_suf[...] = per_piece(after[0:1, :])
+
+    def score_tables():
+        v = dt_ref[...].astype(F32) + bias_ref[...]
+        delta = jnp.maximum(v, 0.0) + jnp.log(1.0 + jnp.exp(-jnp.abs(v)))
+        rt_ref[...] = (a_ref[...] - jnp.log2(delta)).T
+        scores = lax.dot_general(c_ref[...], b_ref[...], (((1,), (1,)), ((), ())), preferred_element_type=F32)
+        t_at = lax.broadcasted_iota(jnp.int32, (TOK, TOK), 0)
+        s_at = lax.broadcasted_iota(jnp.int32, (TOK, TOK), 1)
+        sm_ref[...] = jnp.where(t_at >= s_at, scores, 0.0)
 
     lane = lax.broadcasted_iota(jnp.int32, (TOK, 128), 1)
     first = lane < HDIM
@@ -140,45 +166,61 @@
     def columns_of(q):
         return pl.ds(pl.multiple_of(q * 128, 128), 128)
 
-    def local_state(q):
-        spread = (pick_head == 2 * q + pick_lane).astype(BF16)
+    wide_head = lax.broadcasted_iota(jnp.int32, (128, 128 * BATCH), 0)
+    wide_lane = lax.broadcasted_iota(jnp.int32, (128, 128 * BATCH), 1) // HDIM
+
+    def local_states(q):
+        cols = pl.ds(pl.multiple_of(q * 128, 128 * BATCH), 128 * BATCH)
+        spread = (wide_head == 2 * q + wide_lane).astype(BF16)
         gain = jnp.dot(g_ref[...], spread, preferred_element_type=F32)
-        scaled = (x_ref[:, columns_of(q)].astype(F32) * gain).astype(BF16)
-        l_ref[q] = jnp.dot(bt_ref[...], scaled, preferred_element_type=F32).astype(BF16)
-
-    def within_and_skip(q):
-        x = x_ref[:, columns_of(q)]
-        turned = pltpu.roll(a_ref[...], lax.rem(HEADS - 2 * q, HEADS), 1)
-        columns, parts = [], []
-        for k in range(2):
-            column = jnp.broadcast_to(turned[:, k : k + 1], (TOK, 128))
-            columns.append(column)
-            row = rt_ref[pl.ds(2 * q + k, 1), :]
-            outs = []
-            for t0, t1 in ((0, 128), (128, 256), (256, TOK)):
-                tiles = []
-                for s0 in range(0, t1, 128):
-                    s1 = min(s0 + 128, t1)
-                    gap = column[t0:t1, : s1 - s0] - row[:, s0:s1]
-                    if s1 > t0:
-                        gap = jnp.minimum(gap, 100.0)
-                    tiles.append((sm_ref[t0:t1, s0:s1] * jnp.exp2(gap)).astype(BF16))
-                w = jnp.concatenate(tiles, axis=1) if len(tiles) > 1 else tiles[0]
-                outs.append(jnp.dot(w, x[:t1], preferred_element_type=F32))
-            parts.append(jnp.concatenate(outs, axis=0))
-        fade_ref[q] = jnp.exp2(jnp.where(first, columns[0], columns[1]))
-        skip = jnp.where(first, skip_ref[0, 2 * q], skip_ref[0, 2 * q + 1])
-        part_ref[q] = jnp.where(first, parts[0], parts[1]) + skip * x.astype(F32)
-
-    def finish(q):
-        carried = jnp.dot(c_ref[...], fl[q], preferred_element_type=F32)
-        o_ref[:, columns_of(q)] = (part_ref[q] + fade_ref[q] * carried).astype(BF16)
-        pltpu.make_async_copy(o_ref.at[:, columns_of(q)], o_hbm.at[:, columns_of(q)], o_sem).start()
+        scaled = (x_ref[:, cols].astype(F32) * gain).astype(BF16)
+        state = jnp.dot(bt_ref[...], scaled, preferred_element_type=F32).astype(BF16)
+        for u in range(BATCH):
+            l_ref[q + u] = state[:, 128 * u : 128 * (u + 1)]
+
+    def within_and_skip(start):
+        turned = pltpu.roll(a_ref[...], lax.rem(HEADS - 2 * start, HEADS), 1)
+        for u in range(2):
+            q = start + u
+            x = x_ref[:, columns_of(q)]
+            columns, parts = [], []
+            for k in range(2):
+                h = 2 * u + k
+                column = jnp.broadcast_to(turned[:, h : h + 1], (TOK, 128))
+                columns.append(column)
+                row = rt_ref[pl.ds(2 * q + k, 1), :]
+                outs = []
+                for t0, t1 in ((0, 128), (128, 256), (256, TOK)):
+                    tiles = []
+                    for s0 in range(0, t1, 128):
+                        s1 = min(s0 + 128, t1)
+                        gap = column[t0:t1, : s1 - s0] - row[:, s0:s1]
+                        if s1 > t0:
+                            gap = jnp.minimum(gap, 100.0)
+                        tiles.append((sm_ref[t0:t1, s0:s1] * jnp.exp2(gap)).astype(BF16))
+                    w = jnp.concatenate(tiles, axis=1) if len(tiles) > 1 else tiles[0]
+                    outs.append(jnp.dot(w, x[:t1], preferred_element_type=F32))
+                parts.append(jnp.concatenate(outs, axis=0))
+            fade_ref[q] = jnp.exp2(jnp.where(first, columns[0], columns[1]))
+            skip = jnp.where(first, skip_ref[0, 2 * q], skip_ref[0, 2 * q + 1])
+            part_ref[q] = jnp.where(first, parts[0], parts[1]) + skip * x.astype(F32)
+
+    def finish(start):
+        both = jnp.concatenate([fl[start], fl[start + 1]], axis=1)
+        carried = jnp.dot(c_ref[...], both, preferred_element_type=F32)
+        for u in range(2):
+            q = start + u
+            here = part_ref[q] + fade_ref[q] * carried[:, 128 * u : 128 * (u + 1)]
+            o_ref[:, columns_of(q)] = here.astype(BF16)
 
     def tick(i, carry):
+        @pl.when(i == MEET)
+        def _():
+            meet_row()
+
         for par in range(2):
             m = low + par
-            q = i - (4 * A + B + C) - A * jnp.abs(z - m)
+            q = i - (4 * A + B + C) - AO * jnp.abs(z - m)
             at = jnp.clip(q, 0, K - 1)
             k = at // 2
             valid = (q >= 0) & (q < K) & (lax.rem(at, 2) == par)
@@ -198,7 +240,7 @@
 
             @pl.when(valid & (z == m))
             def _():
-                mine = r // PARTS == lax.rem(k, R // PARTS)
+                mine = group == lax.rem(k, groups)
 
                 @pl.when(mine)
                 def _():
@@ -230,9 +272,9 @@
         def _():
             x_copy(ahead // per_block).wait()
 
-        @pl.when(i < K)
-        def _():
-            local_state(ahead)
+        @pl.when((i < K) & (lax.rem(ahead, BATCH) == 0))
+        def _():
+            local_states(pl.multiple_of(ahead, BATCH))
 
         q = i - A * z
         at = jnp.clip(q, 0, K - 1)
@@ -274,10 +316,9 @@
             total = (dec_suf[pl.ds(at2, 1), :] * inner + fr[at2].astype(F32)).astype(BF16)
 
             rs[k2] = total
-            base = lax.rem(k2, R // PARTS) * PARTS
-            turn = k2 // (R // PARTS)
+            turn = k2 // groups
             for p in range(PARTS):
-                to = base + p
+                to = owner(lax.rem(k2, groups), p)
 
                 @pl.when(to == r)
                 def _():
@@ -296,7 +337,7 @@
             await_bytes(pa.at[0 : 8 * (R - 1), :], p_recv)
 
         for turn in range(TURNS):
-            k3 = r // PARTS + turn * (R // PARTS)
+            k3 = group + turn * groups
             q3 = 2 * k3 + (z - low)
 
             @pl.when(in_plane & (i == q3 + 4 * A + B))
@@ -328,26 +369,31 @@
 
                 lax.fori_loop(0, R, row, jnp.zeros((rows, 128), F32))
 
-        w = i // 3 * 2 + lax.rem(i, 3)
-        w_at = jnp.minimum(w, K - 1)
-
-        @pl.when((lax.rem(i, 3) < 2) & (w < K))
-        def _():
-            within_and_skip(w_at)
-
-        for par in range(2):
-            q = i - (4 * A + B + C) - A * jnp.abs(z - low - par)
-            at = jnp.clip(q, 0, K - 1)
-
-            @pl.when((q >= 0) & (q < K) & (lax.rem(at, 2) == par))
-            def _():
-                finish(at)
+        @pl.when(i == 0)
+        def _():
+            score_tables()
+
+        early = FILL // 2
+        w = jnp.where(i < FILL, i // 2, early + (i - FILL) // 4)
+        now = jnp.where(i < FILL, lax.rem(i, 2) == 0, lax.rem(i, 4) == 0)
+        w_at = jnp.minimum(w, K // 2 - 1)
+
+        @pl.when(now & (w < K // 2))
+        def _():
+            within_and_skip(2 * w_at)
+
+        far = jnp.maximum(jnp.abs(z - low), jnp.abs(z - low - 1))
+        done = i - (4 * A + B + C) - AO * far - 1
+        done_at = jnp.clip(done, 0, K - 2)
+
+        @pl.when((done >= 0) & (done < K - 1) & (lax.rem(done_at, 2) == 0))
+        def _():
+            finish(done_at)
 
         return carry
 
-    lax.fori_loop(0, K + 4 * A + B + C + A * (Z // 2), tick, 0)
-
-    pltpu.make_async_copy(o_ref, o_hbm, o_sem).wait()
+    lax.fori_loop(0, K + 4 * A + B + C + AO * (Z // 2), tick, 0)
+
     await_bytes(za.at[0 : 8 * (Z - 1), :], z_send)
 
     @pl.when(z > 0)
@@ -366,7 +412,7 @@
             await_bytes(rbuf.at[turn, 0 : R - 1], eb_sem)
 
 
-def layer_call(x, b, c, dt, bias, alog, skip, Z=8, K=PIECES, A=6, B=8, C=10):
+def layer_call(x, b, c, dt, bias, alog, skip, Z=8, K=PIECES, A=6, AO=6, B=8, C=10):
     Y = lax.axis_size("head") // Z
     R = lax.axis_size("seq") * Y
     tile = (DSTATE, 128)
@@ -376,12 +422,11 @@
     small = pltpu.VMEM((R * 8, 128), F32)
     share = pltpu.VMEM((TURNS, R, DSTATE // PARTS, 128), BF16)
     return pl.pallas_call(
-        functools.partial(layer_kernel, (Z, Y, R, K, A, B, C)),
+        functools.partial(layer_kernel, (Z, Y, R, K, A, AO, B, C)),
         in_specs=[hbm, vmem, vmem, vmem, vmem, vmem, pl.BlockSpec(memory_space=pltpu.SMEM)],
-        out_specs=hbm,
-        out_shape=jax.ShapeDtypeStruct((TOK, K * 128), BF16),
+        out_specs=vmem,
+        out_shape=pltpu.VMEM((TOK, K * 128), BF16) if K == PIECES else jax.ShapeDtypeStruct((TOK, K * 128), BF16),
         scratch_shapes=[
-            pltpu.VMEM((TOK, K * 128), BF16),
             pltpu.VMEM((TOK, K * 128), BF16),
             pltpu.VMEM((K, TOK, 128), F32),
             pltpu.VMEM((K, TOK, 128), F32),
@@ -405,7 +450,7 @@
             pltpu.VMEM((K, 128), F32),
             pltpu.VMEM((K, 128), F32),
             small,
-            dma((XBLOCKS,)), dma, dma((K,)), dma((K,)), dma((K // 2,)),
+            dma((XBLOCKS,)), dma((K,)), dma((K,)), dma((K // 2,)),
             dma, dma, dma, dma((TURNS,)), dma, dma, dma, dma, dma,
         ],
         compiler_params=pltpu.CompilerParams(
@@ -415,8 +460,27 @@
     )(x, b, c, dt, bias, alog, skip)
 
 
+def store_kernel(y_ref, o_hbm, sem):
+    copy = pltpu.make_async_copy(y_ref, o_hbm, sem)
+    copy.start()
+    copy.wait()
+
+
+def store_call(y):
+    return pl.pallas_call(
+        store_kernel,
+        in_specs=[pl.BlockSpec(memory_space=pltpu.VMEM)],
+        out_specs=pl.BlockSpec(memory_space=pl.ANY),
+        out_shape=jax.ShapeDtypeStruct(y.shape, y.dtype),
+        scratch_shapes=[pltpu.SemaphoreType.DMA],
+        compiler_params=pltpu.CompilerParams(vmem_limit_bytes=8 * 1024 * 1024),
+        name="store",
+    )(y)
+
+
 def on_device(inputs, b_panel, c_panel, dt_raw, dt_bias, a_log, d_skip):
-    return layer_call(inputs, b_panel, c_panel, dt_raw, dt_bias[None], a_log[None], d_skip[None])
+    y = layer_call(inputs, b_panel, c_panel, dt_raw, dt_bias[None], a_log[None], d_skip[None])
+    return store_call(y)
 
 
 def solution(mesh):

time: 123 us -> 102 us (0.83)
  Pallas kernels: 118 us -> 102 us
  local copies, waits for them, and re-layouts: 5.43 us -> 0 us
    pallas_call x1 -> x2, Pallas kernels: 118 us -> 102 us  [the longest x1 99.7 us: layer_call(): pl.pallas_call(functools.partial(layer_kernel, (Z, Y, R, K, A, AO, B, C))...]
    unnamed x1 -> x0, local copies, waits for them, and re-layouts: 5.43 us -> none
where the time goes in v4:
time: 102 us
  Pallas kernels  102 us (100%)
    pallas_call x1, Pallas kernels, layer_call(): pl.pallas_call(functools.partial(layer_kernel, (Z, Y, R, K, A, AO, B, C))...  99.7 us
    pallas_call x1, Pallas kernels, store_call(): pl.pallas_call(store_kernel, in_specs=[pl.BlockSpec(memory_space=pltpu.VM...  2.37 us

profile of v4, /device:TPU:1, one launch (start us, length us, event | category | flops | bytes accessed | tf_op | source)
XLA Modules:
  0.0 102.1 jit_solution(17915481906454720988)
XLA Ops:
  0.0 99.7 %layer.1.y_ref = bf16[320,8192]{1,0:T(8,128)(2,1)S(1)} custom-call(bf16[320,8192]{1,0:T(8,128)(2,1)} %x_hbm.1, bf16[320,128]{1,0:T(8,128)(2,1)} %b_ref.1, bf16[320,128]{1,0:T(8,128)(2,1)} %c_ref.1, bf16[320,128]{1,0:T(8,128)(2,1)} %dt_ref.1, f32[1,128]{1,0:T(1,128)} %bitcast.3, f32[1,128]{1,0:T(1,128)} %bitcast.4, f32[1,128]{1,0:T(1,128)} %bitcast.5), custom_call_target="tpu_custom_call" | custom-call | tf_op jit(solution)/shard_map/layer/pallas_call | solution.py:424
  99.7 2.4 %store.1 = bf16[320,8192]{1,0:T(8,128)(2,1)} custom-call(bf16[320,8192]{1,0:T(8,128)(2,1)S(1)} %layer.1.y_ref), custom_call_target="tpu_custom_call" | custom-call | tf_op jit(solution)/shard_map/store/pallas_call | solution.py:470

commit v5 on v4

--- a/solution.py
+++ b/solution.py
@@ -18,16 +18,18 @@
 BATCH = 4
 FILL = 24
 MEET = 5
+STORES = 4
 LOG2E = 1.4426950408889634
 F32 = jnp.float32
 BF16 = jnp.bfloat16
 VMEM_LIMIT = 56 * 1024 * 1024
 
 
-def layer_kernel(cfg, x_hbm, b_ref, c_ref, dt_ref, bias_ref, alog_ref, skip_ref, o_ref,
+def layer_kernel(cfg, x_hbm, b_hbm, c_hbm, dt_hbm, bias_hbm, alog_hbm, skip_hbm, o_ref,
+                 b_ref, c_ref, dt_ref, bias_ref, alog_ref, skip_ref, skips,
                  x_ref, part_ref, fade_ref, a_ref, rt_ref, sm_ref, g_ref, bt_ref,
                  l_ref, fl, fr, fe, sl, sr, rs, rbuf, eb, za, pa, dec_own, dec_pre, dec_suf, rowdec,
-                 x_sem, fl_sem, fr_sem, fe_sem, left_sem, right_sem, rs_sem, rbuf_sem, eb_sem,
+                 in_sem, x_sem, fl_sem, fr_sem, fe_sem, left_sem, right_sem, rs_sem, rbuf_sem, eb_sem,
                  z_send, z_recv, p_send, p_recv):
     Z, Y, R, K, A, AO, B, C = cfg
     low = Z // 2 - 1
@@ -62,6 +64,11 @@
     def send_right(src, q):
         remote(src, fl.at[q], right_sem, fl_sem.at[q], seq, head + 1).start()
 
+    pairs = ((b_hbm, b_ref), (c_hbm, c_ref), (dt_hbm, dt_ref), (bias_hbm, bias_ref), (alog_hbm, alog_ref), (skip_hbm, skip_ref))
+    loads = [pltpu.make_async_copy(src, dst, in_sem.at[n]) for n, (src, dst) in enumerate(pairs)]
+    for copy in loads:
+        copy.start()
+
     gate = pltpu.get_barrier_semaphore()
 
     def greet(to_seq, to_head):
@@ -91,6 +98,9 @@
 
     for n in range(blocks):
         x_copy(n).start()
+
+    for copy in loads:
+        copy.wait()
 
     v = dt_ref[...].astype(F32) + bias_ref[...]
     delta = jnp.maximum(v, 0.0) + jnp.log(1.0 + jnp.exp(-jnp.abs(v)))
@@ -112,9 +122,9 @@
         second = (lax.rem(pick_head, 2) == pick_lane).astype(F32)
         only = jnp.where(head_at // 2 == piece_at, value, 0.0)
         logs = jnp.dot(only, second, precision=lax.Precision.HIGHEST, preferred_element_type=F32)
-        return jnp.exp2(logs)
-
-    dec_own[...] = per_piece(a[TOK - 1 : TOK, :])
+        return logs
+
+    dec_own[...] = jnp.exp2(per_piece(a[TOK - 1 : TOK, :]))
     my_row = pl.ds(pl.multiple_of(z * 8, 8), 8)
     za[my_row, :] = jnp.broadcast_to(a[TOK - 1 : TOK, :], (8, 128))
 
@@ -148,8 +158,8 @@
 
             lax.fori_loop(1, R, tell, 0)
 
-        dec_pre[...] = per_piece(before[0:1, :])
-        dec_suf[...] = per_piece(after[0:1, :])
+        dec_pre[...] = jnp.exp2(per_piece(before[0:1, :]))
+        dec_suf[...] = jnp.exp2(per_piece(after[0:1, :]))
 
     def score_tables():
         v = dt_ref[...].astype(F32) + bias_ref[...]
@@ -159,6 +169,7 @@
         t_at = lax.broadcasted_iota(jnp.int32, (TOK, TOK), 0)
         s_at = lax.broadcasted_iota(jnp.int32, (TOK, TOK), 1)
         sm_ref[...] = jnp.where(t_at >= s_at, scores, 0.0)
+        skips[...] = per_piece(skip_ref[...])
 
     lane = lax.broadcasted_iota(jnp.int32, (TOK, 128), 1)
     first = lane < HDIM
@@ -202,8 +213,7 @@
                     outs.append(jnp.dot(w, x[:t1], preferred_element_type=F32))
                 parts.append(jnp.concatenate(outs, axis=0))
             fade_ref[q] = jnp.exp2(jnp.where(first, columns[0], columns[1]))
-            skip = jnp.where(first, skip_ref[0, 2 * q], skip_ref[0, 2 * q + 1])
-            part_ref[q] = jnp.where(first, parts[0], parts[1]) + skip * x.astype(F32)
+            part_ref[q] = jnp.where(first, parts[0], parts[1]) + skips[pl.ds(q, 1), :] * x.astype(F32)
 
     def finish(start):
         both = jnp.concatenate([fl[start], fl[start + 1]], axis=1)
@@ -412,7 +422,7 @@
             await_bytes(rbuf.at[turn, 0 : R - 1], eb_sem)
 
 
-def layer_call(x, b, c, dt, bias, alog, skip, Z=8, K=PIECES, A=6, AO=6, B=8, C=10):
+def layer_call(x, b, c, dt, bias, alog, skip, Z=8, K=PIECES, A=6, AO=6, B=7, C=8):
     Y = lax.axis_size("head") // Z
     R = lax.axis_size("seq") * Y
     tile = (DSTATE, 128)
@@ -423,10 +433,17 @@
     share = pltpu.VMEM((TURNS, R, DSTATE // PARTS, 128), BF16)
     return pl.pallas_call(
         functools.partial(layer_kernel, (Z, Y, R, K, A, AO, B, C)),
-        in_specs=[hbm, vmem, vmem, vmem, vmem, vmem, pl.BlockSpec(memory_space=pltpu.SMEM)],
+        in_specs=[hbm] * 7,
         out_specs=vmem,
         out_shape=pltpu.VMEM((TOK, K * 128), BF16) if K == PIECES else jax.ShapeDtypeStruct((TOK, K * 128), BF16),
         scratch_shapes=[
+            pltpu.VMEM((TOK, DSTATE), BF16),
+            pltpu.VMEM((TOK, DSTATE), BF16),
+            pltpu.VMEM((TOK, HEADS), BF16),
+            pltpu.VMEM((1, HEADS), F32),
+            pltpu.VMEM((1, HEADS), F32),
+            pltpu.VMEM((1, HEADS), F32),
+            pltpu.VMEM((K, 128), F32),
             pltpu.VMEM((TOK, K * 128), BF16),
             pltpu.VMEM((K, TOK, 128), F32),
             pltpu.VMEM((K, TOK, 128), F32),
@@ -450,7 +467,7 @@
             pltpu.VMEM((K, 128), F32),
             pltpu.VMEM((K, 128), F32),
             small,
-            dma((XBLOCKS,)), dma((K,)), dma((K,)), dma((K // 2,)),
+            dma((6,)), dma((XBLOCKS,)), dma((K,)), dma((K,)), dma((K // 2,)),
             dma, dma, dma, dma((TURNS,)), dma, dma, dma, dma, dma,
         ],
         compiler_params=pltpu.CompilerParams(
@@ -461,9 +478,15 @@
 
 
 def store_kernel(y_ref, o_hbm, sem):
-    copy = pltpu.make_async_copy(y_ref, o_hbm, sem)
-    copy.start()
-    copy.wait()
+    rows = TOK // STORES
+    copies = [
+        pltpu.make_async_copy(y_ref.at[rows * n : rows * (n + 1)], o_hbm.at[rows * n : rows * (n + 1)], sem.at[n])
+        for n in range(STORES)
+    ]
+    for copy in copies:
+        copy.start()
+    for copy in copies:
+        copy.wait()
 
 
 def store_call(y):
@@ -472,7 +495,7 @@
         in_specs=[pl.BlockSpec(memory_space=pltpu.VMEM)],
         out_specs=pl.BlockSpec(memory_space=pl.ANY),
         out_shape=jax.ShapeDtypeStruct(y.shape, y.dtype),
-        scratch_shapes=[pltpu.SemaphoreType.DMA],
+        scratch_shapes=[pltpu.SemaphoreType.DMA((STORES,))],
         compiler_params=pltpu.CompilerParams(vmem_limit_bytes=8 * 1024 * 1024),
         name="store",
     )(y)

time: 102 us -> 101 us (level)
    pallas_call x1, Pallas kernels: 99.7 us -> 98.3 us  [layer_call(): pl.pallas_call(functools.partial(layer_kernel, (Z, Y, R, K, A, AO, B, C))...]
where the time goes in v5:
time: 101 us
  Pallas kernels  101 us (100%)
    pallas_call x1, Pallas kernels, layer_call(): pl.pallas_call(functools.partial(layer_kernel, (Z, Y, R, K, A, AO, B, C))...  98.3 us
    pallas_call x1, Pallas kernels, store_call(): pl.pallas_call(store_kernel, in_specs=[pl.BlockSpec(memory_space=pltpu.VM...  2.39 us

profile of v5, /device:TPU:1, one launch (start us, length us, event | category | flops | bytes accessed | tf_op | source)
XLA Modules:
  0.0 100.7 jit_solution(11805493876325634217)
XLA Ops:
  0.0 98.3 %layer.1.y_ref = bf16[320,8192]{1,0:T(8,128)(2,1)S(1)} custom-call(bf16[320,8192]{1,0:T(8,128)(2,1)} %x_hbm.1, bf16[320,128]{1,0:T(8,128)(2,1)} %b_hbm.1, bf16[320,128]{1,0:T(8,128)(2,1)} %c_hbm.1, bf16[320,128]{1,0:T(8,128)(2,1)} %dt_hbm.1, f32[1,128]{1,0:T(1,128)} %bitcast.3, f32[1,128]{1,0:T(1,128)} %bitcast.4, f32[1,128]{1,0:T(1,128)} %bitcast.5), custom_call_target="tpu_custom_call" | custom-call | tf_op jit(solution)/shard_map/layer/pallas_call | solution.py:434
  98.3 2.4 %store.1 = bf16[320,8192]{1,0:T(8,128)(2,1)} custom-call(bf16[320,8192]{1,0:T(8,128)(2,1)S(1)} %layer.1.y_ref), custom_call_target="tpu_custom_call" | custom-call | tf_op jit(solution)/shard_map/store/pallas_call | solution.py:493

commit v6 on v5

--- a/solution.py
+++ b/solution.py
@@ -107,8 +107,13 @@
     rates = (-LOG2E) * jnp.exp(alog_ref[...]) * delta
     t_at = lax.broadcasted_iota(jnp.int32, (TOK, TOK), 0)
     s_at = lax.broadcasted_iota(jnp.int32, (TOK, TOK), 1)
-    lower = (t_at >= s_at).astype(F32)
-    a = jnp.dot(lower, rates, precision=lax.Precision.HIGHEST, preferred_element_type=F32)
+    lower = (t_at >= s_at).astype(BF16)
+    high = rates.astype(BF16)
+    rest_1 = rates - high.astype(F32)
+    mid = rest_1.astype(BF16)
+    fine = (rest_1 - mid.astype(F32)).astype(BF16)
+    sums = jnp.dot(lower, jnp.concatenate([high, mid, fine], axis=1), preferred_element_type=F32)
+    a = sums[:, :HEADS] + (sums[:, HEADS : 2 * HEADS] + sums[:, 2 * HEADS :])
     a_ref[...] = a
     g_ref[...] = (jnp.exp2(a[TOK - 1 : TOK, :] - a) * delta).astype(BF16)
     bt_ref[...] = b_ref[...].astype(F32).T.astype(BF16)

time: 101 us -> 101 us (level)
  no operation moved by 1% of the time
where the time goes in v6:
time: 101 us
  Pallas kernels  101 us (100%)
    pallas_call x1, Pallas kernels, layer_call(): pl.pallas_call(functools.partial(layer_kernel, (Z, Y, R, K, A, AO, B, C))...  98.7 us
    pallas_call x1, Pallas kernels, store_call(): pl.pallas_call(store_kernel, in_specs=[pl.BlockSpec(memory_space=pltpu.VM...  2.39 us

profile of v6, /device:TPU:1, one launch (start us, length us, event | category | flops | bytes accessed | tf_op | source)
XLA Modules:
  0.0 101.1 jit_solution(13344759347733876570)
XLA Ops:
  0.0 98.7 %layer.1.y_ref = bf16[320,8192]{1,0:T(8,128)(2,1)S(1)} custom-call(bf16[320,8192]{1,0:T(8,128)(2,1)} %x_hbm.1, bf16[320,128]{1,0:T(8,128)(2,1)} %b_hbm.1, bf16[320,128]{1,0:T(8,128)(2,1)} %c_hbm.1, bf16[320,128]{1,0:T(8,128)(2,1)} %dt_hbm.1, f32[1,128]{1,0:T(1,128)} %bitcast.3, f32[1,128]{1,0:T(1,128)} %bitcast.4, f32[1,128]{1,0:T(1,128)} %bitcast.5), custom_call_target="tpu_custom_call" | custom-call | tf_op jit(solution)/shard_map/layer/pallas_call | solution.py:439
  98.7 2.4 %store.1 = bf16[320,8192]{1,0:T(8,128)(2,1)} custom-call(bf16[320,8192]{1,0:T(8,128)(2,1)S(1)} %layer.1.y_ref), custom_call_target="tpu_custom_call" | custom-call | tf_op jit(solution)/shard_map/store/pallas_call | solution.py:498
